TPU v7x, 32 devices: a whole 2x2x4 slice. The times are simulated.
32 devices in a mesh: cam: 16 (over z, x, core), depth: 2 (over y).
Axes of the slice: x: 2, y: 2, z: 4, core: 2. Of those that a mesh axis runs over, the one named last changes fastest.
Arguments:
- features: bfloat16 [16, 32, 8, 512], P('cam'), may hold values from -6 to 6
- view_mask: int32 [16, 4], P('cam'), may hold values 0 or 1
- row_offset: int32 [16, 4, 8], P('cam', None, 'depth'), may hold values from 0 to 3
- frac_row: float32 [16, 4, 8], P('cam', None, 'depth'), may hold values from 0 to 1
- col_offset: int32 [16, 4, 8], P('cam', None, 'depth'), may hold values from -32 to 32
- frac_col: float32 [16, 4, 8], P('cam', None, 'depth'), may hold values from 0 to 1
- first_kernel: bfloat16 [8, 32, 3, 3, 3], replicated, may hold values from -0.21875 to 0.21875
- first_bias: float32 [8], replicated, may hold values from -0.5 to 0.5
- second_kernel: bfloat16 [8, 8, 3, 3, 3], replicated, may hold values from -0.4375 to 0.4375
- cotangent: bfloat16 [16, 8, 8, 4, 512], P('cam', None, 'depth'), may hold values from -6 to 6
Outputs:
- feature_grad: float32 [16, 32, 8, 512], P('cam', 'depth')
- first_grad: float32 [8, 32, 3, 3, 3], replicated
- second_grad: float32 [8, 8, 3, 3, 3], replicated
All inputs are finite; a program needn't handle non-finite values. No bound on the sum of `view_mask` on one device may be relied on, other than what follows from the above.
Results may differ from a plain program's by a relative error of at most 0.0053.
Values may be sent and summed in bfloat16 or wider, within the bound.
A program may use at most 128 MiB of HBM per device.

v0:
```python
import jax
import jax.numpy as jnp
from jax import lax
from jax.sharding import PartitionSpec as P

W = 512
D = 8
H = 4
SPAN = 4
SHIFT = 32


view_offsets = (-2, -1, 1, 2)


def from_behind(x, axis, by):
    size = lax.axis_size(axis)
    return lax.ppermute(x, axis, [(i, (i + by) % size) for i in range(size)])


def extended(cells, sides, width):
    for axis, dim in sides:
        count = lax.axis_size(axis)
        ends = count - 1
        head = lax.slice_in_dim(cells, 0, width, axis=dim)
        tail = lax.slice_in_dim(cells, cells.shape[dim] - width, cells.shape[dim], axis=dim)
        cells = jnp.concatenate(
            [
                lax.ppermute(tail, axis, [(i, (i + 1) % count) for i in range(ends)]),
                cells,
                lax.ppermute(head, axis, [((i + 1) % count, i) for i in range(ends)]),
            ],
            axis=dim,
        )
    return cells


def conv_same(volume, kernel, depth_pad):
    return lax.conv_general_dilated(
        volume[None],
        kernel,
        (1, 1, 1),
        [depth_pad, (1, 1), (1, 1)],
        dimension_numbers=("NCDHW", "OIDHW", "NCDHW"),
        preferred_element_type=jnp.float32,
    )[0]


def flipped(kernel):
    return jnp.transpose(jnp.flip(kernel, (2, 3, 4)), (1, 0, 2, 3, 4))


def silu_slope(value):
    gate = jax.nn.sigmoid(value)
    return gate * (1.0 + value * (1.0 - gate))


def pad_source(src_band):
    return jnp.pad(src_band.astype(jnp.float32), ((0, 0), (0, 0), (SHIFT, SHIFT + 1)))


def plane_warp(padded, row_start, col_start, frac_r, frac_c):
    window = lax.dynamic_slice(
        padded,
        (jnp.zeros((), jnp.int32), row_start, col_start + SHIFT),
        (padded.shape[0], H + 1, W + 1),
    )
    row_mixed = (1.0 - frac_r) * window[:, :H, :] + frac_r * window[:, 1:, :]
    return (1.0 - frac_c) * row_mixed[:, :, :W] + frac_c * row_mixed[:, :, 1:]


def slot_warp(padded, row_starts, col_starts, fracs_r, fracs_c):
    return jax.vmap(plane_warp, in_axes=(None, 0, 0, 0, 0), out_axes=1)(
        padded, row_starts, col_starts, fracs_r, fracs_c
    )


def weight_term(volume, grad_out):
    result = lax.conv_general_dilated(
        volume[:, None],
        grad_out[:, None],
        (1, 1, 1),
        [(0, 0), (1, 1), (1, 1)],
        dimension_numbers=("NCDHW", "OIDHW", "NCDHW"),
        preferred_element_type=jnp.float32,
    )
    return jnp.transpose(result, (1, 0, 2, 3, 4))


def send_back(slot_grads, own_part):
    summed = own_part
    for offset in view_offsets:
        summed = summed + from_behind(slot_grads[offset], "cam", offset)
    return summed


def shards(
    features,
    view_mask,
    row_offset,
    frac_row,
    col_offset,
    frac_col,
    first_kernel,
    first_bias,
    second_kernel,
    cotangent,
):
    own_band = features[0]
    top_row = SPAN // 2
    fetched = {}
    for offset in view_offsets:
        fetched[offset] = from_behind(own_band, "cam", -offset)
    rows_use = row_offset[0]
    cols_use = col_offset[0]
    fracs_r = frac_row[0]
    fracs_c = frac_col[0]
    reference_view = own_band[:, top_row : top_row + H, :].astype(jnp.float32)[:, None]
    view_weights = view_mask[0].astype(jnp.float32)
    view_count = 1.0 + jnp.sum(view_weights)
    first_moment = reference_view
    second_moment = reference_view * reference_view
    paddings, warps = ({}, {})
    for slot_id, offset in enumerate(view_offsets):
        padded = pad_source(fetched[offset])
        warped = slot_warp(
            padded, rows_use[slot_id], cols_use[slot_id], fracs_r[slot_id], fracs_c[slot_id]
        )
        first_moment = first_moment + view_weights[slot_id] * warped
        second_moment = second_moment + view_weights[slot_id] * (warped * warped)
        paddings[offset] = padded
        warps[offset] = warped
    mean_full = first_moment / view_count
    cost_raw = second_moment / view_count - mean_full * mean_full
    cost_volume = cost_raw.astype(jnp.bfloat16)
    cost_ext = extended(cost_volume, (("depth", 1),), 1)
    pre_act = conv_same(cost_ext, first_kernel, (0, 0)) + first_bias[:, None, None, None]
    hidden = jax.nn.silu(pre_act).astype(jnp.bfloat16)
    hidden_ext = extended(hidden, (("depth", 1),), 1)
    cot_local = cotangent[0]
    cot_ext = extended(cot_local, (("depth", 1),), 1)
    hidden_grad = conv_same(cot_ext, flipped(second_kernel), (0, 0))
    pre_grad = (hidden_grad * silu_slope(pre_act)).astype(jnp.bfloat16)
    pre_ext = extended(pre_grad, (("depth", 1),), 1)
    cost_grad = conv_same(pre_ext, flipped(first_kernel), (0, 0))
    first_term = weight_term(cost_ext, pre_grad)
    second_term = weight_term(hidden_ext, cot_local)
    scaled = 2.0 * cost_grad / view_count
    ref_grad = jnp.sum(scaled * (reference_view - mean_full), axis=1)
    own_part = jnp.pad(ref_grad, ((0, 0), (top_row, SPAN - top_row), (0, 0)))
    slot_grads = {}
    for slot_id, offset in enumerate(view_offsets):
        slot_grad = view_weights[slot_id] * scaled * (warps[offset] - mean_full)
        outcome, pullback = jax.vjp(
            lambda padded_src: slot_warp(
                padded_src,
                row_offset[0, slot_id],
                col_offset[0, slot_id],
                frac_row[0, slot_id],
                frac_col[0, slot_id],
            ),
            paddings[offset],
        )
        slot_grads[offset] = pullback(slot_grad)[0][:, :, SHIFT : SHIFT + W]
    summed = send_back(slot_grads, own_part)
    feature_grad = lax.psum_scatter(summed, "depth", scatter_dimension=0, tiled=True)
    first_sum, second_sum = lax.psum((first_term, second_term), ("cam", "depth"))
    grad_scale = (lax.axis_size("cam") * D * H * W) ** (-0.5)
    return (feature_grad[None], first_sum * grad_scale, second_sum * grad_scale)


def solution(mesh):
    placed = (
        P("cam", None, None, None),
        P("cam", None),
        P("cam", None, "depth"),
        P("cam", None, "depth"),
        P("cam", None, "depth"),
        P("cam", None, "depth"),
        P(),
        P(),
        P(),
        P("cam", None, "depth", None, None),
    )
    return jax.shard_map(
        shards,
        mesh=mesh,
        in_specs=placed,
        out_specs=(P("cam", "depth", None, None), P(), P()),
        check_vma=False,
    )
```

profile of v0, /device:TPU:0, one launch (start us, length us, event | category | flops | bytes accessed | tf_op | source)
XLA Modules:
  0.0 633.7 jit_solution(1394594515668619876)
XLA Ops:
  9.0 6.0 collective-permute-start.5
  35.6 7.3 %copy.206 = bf16[8,1,4,4,512]{0,1,4,3,2:T(2,128)(2,1)} copy(bf16[8,1,4,4,512]{4,3,2,0,1:T(4,128)(2,1)S(1)} %bitcast.321) | data formatting | bytes 262144 | tf_op jit(solution)/shard_map/broadcast_in_dim;squeeze | solution.py:81
  46.2 4.2 collective-permute-start.4
  58.5 12.0 %while.11 = (s32[]{:T(128)}, f32[32,8,577]{2,0,1:T(8,128)S(1)}, s32[4,3]{1,0:T(4,128)}, f32[4,32,5,513]{3,1,2,0:T(8,128)S(1)}, s32[]{:T(128)}) while((s32[]{:T(128)}, f32[32,8,577]{2,0,1:T(8,128)S(1)}, s32[4,3]{1,0:T(4,128)}, f32[4,32,5,513]{3,1,2,0:T(8,128)S(1)}, s32[]{:T(128)}) %tuple.239), condition=%wide.while_cond.3, body=%wide.while_body.3.sunk | while | flops 2 | bytes 2378357 | solution.py:63
  73.1 15.2 %while.9 = (s32[]{:T(128)}, f32[32,8,577]{2,0,1:T(8,128)S(1)}, s32[4,3]{1,0:T(4,128)}, f32[4,32,5,513]{3,1,2,0:T(8,128)}, s32[]{:T(128)}) while((s32[]{:T(128)}, f32[32,8,577]{2,0,1:T(8,128)S(1)}, s32[4,3]{1,0:T(4,128)}, f32[4,32,5,513]{3,1,2,0:T(8,128)}, s32[]{:T(128)}) %tuple.233), condition=%wide.while_cond.1, body=%wide.while_body.1.sunk | while | flops 2 | bytes 2051825 | solution.py:63
  90.8 15.4 %while.8 = (s32[]{:T(128)}, f32[32,8,577]{2,0,1:T(8,128)S(1)}, s32[4,3]{1,0:T(4,128)}, f32[4,32,5,513]{3,1,2,0:T(8,128)}, s32[]{:T(128)}) while((s32[]{:T(128)}, f32[32,8,577]{2,0,1:T(8,128)S(1)}, s32[4,3]{1,0:T(4,128)}, f32[4,32,5,513]{3,1,2,0:T(8,128)}, s32[]{:T(128)}) %tuple.230), condition=%wide.while_cond, body=%wide.while_body.sunk | while | flops 2 | bytes 2051825 | solution.py:63
  108.8 15.3 %while.10 = (s32[]{:T(128)}, f32[32,8,577]{2,0,1:T(8,128)S(1)}, s32[4,3]{1,0:T(4,128)}, f32[4,32,5,513]{3,1,2,0:T(8,128)}, s32[]{:T(128)}) while((s32[]{:T(128)}, f32[32,8,577]{2,0,1:T(8,128)S(1)}, s32[4,3]{1,0:T(4,128)}, f32[4,32,5,513]{3,1,2,0:T(8,128)}, s32[]{:T(128)}) %tuple.236), condition=%wide.while_cond.2, body=%wide.while_body.2.sunk | while | flops 2 | bytes 2051825 | solution.py:63
  130.5 6.2 subtract_convert_fusion
  136.6 4.3 collective-permute-start.6
  142.5 7.4 %broadcast_select_fusion.1 = f32[4,4,8,65,8]{4,2,3,1,0:T(8,128)} fusion(pred[8,65]{0,1:T(8,128)(4,1)S(1)} %copy-done.39, bf16[8,8,3,3,3]{1,0,4,3,2:T(8,128)(2,1)S(1)} %copy-done.38, bf16[8,6,4,1,7,2]{0,4,5,2,1,3:T(8,128)(2,1)S(1)} %copy-done.15, bf16[8,6,4,1,8,65]{0,4,5,2,1,3:T(8,128)(2,1)S(1)} %copy-done.6), kind=kOutput, calls=%fused_computation.64 | convolution fusion | flops 24645632 | bytes 475272 | tf_op jit(solution)/shard_map/conv_general_dilated | solution.py:39
  160.9 11.0 %broadcast_select_fusion = f32[4,4,8,65,8]{4,2,3,1,0:T(8,128)} fusion(pred[8,65]{0,1:T(8,128)(4,1)S(1)} %copy-done.40, bf16[8,32,3,3,3]{1,0,4,3,2:T(8,128)(2,1)S(1)} %copy-done, bf16[32,6,4,1,7,2]{0,4,5,2,1,3:T(8,128)(2,1)S(1)} %slice.393, bf16[32,6,4,1,8,65]{0,4,5,2,1,3:T(8,128)(2,1)} %copy.185), kind=kOutput, calls=%fused_computation.63 | convolution fusion | flops 98382848 | bytes 1100808 | tf_op jit(solution)/shard_map/conv_general_dilated | solution.py:39
  175.7 4.6 collective-permute-start.8
  182.2 4.5 collective-permute-start.14
  188.0 7.7 %copy.204 = bf16[8,1,4,4,512]{0,1,4,3,2:T(2,128)(2,1)} copy(bf16[8,1,4,4,512]{4,0,3,2,1:T(8,128)(2,1)S(1)} %fusion.49) | data formatting | bytes 262144 | tf_op jit(solution)/shard_map/convert_element_type | solution.py:143
  195.8 10.7 %copy.203 = bf16[32,1,6,4,512]{0,1,4,3,2:T(2,128)(2,1)} copy(bf16[32,1,6,4,512]{4,0,3,2,1:T(8,128)(2,1)S(1)} %get-tuple-element.358) | data formatting | bytes 1572864 | tf_op jit(solution)/shard_map/broadcast_in_dim | solution.py:80
  211.3 7.4 %fusion.13 = f32[4,4,8,65,32]{4,2,3,1,0:T(8,128)} fusion(bf16[8,32,3,3,3]{1,0,4,3,2:T(8,128)(2,1)S(1)} %copy-done, bf16[8,6,4,1,7,2]{0,4,5,2,1,3:T(8,128)(2,1)S(1)} %slice.397, bf16[8,6,4,1,8,65]{0,4,5,2,1,3:T(8,128)(2,1)S(1)} %copy.188), kind=kOutput, calls=%fused_computation.53 | convolution fusion | flops 96463872 | bytes 1283840 | tf_op jit(solution)/shard_map/conv_general_dilated | solution.py:39
  218.7 3.7 copy.189
  225.1 9.0 %multiply_bitcast_fusion.7 = (f32[4,32,4,512]{3,1,2,0:T(8,128)S(1)}, f32[32,4,4,512]{3,0,2,1:T(8,128)S(1)}, f32[32,4,512]{2,0,1:T(8,128)}, f32[4,32,4,512]{3,1,2...) fusion(f32[4]{0:T(128)S(1)} %copy-done.33, ...), kind=kLoop, calls=%fused_computation.108 | loop fusion | flops 4915200 | bytes 15204432 | tf_op jit(solution)/shard_map/transpose(jvp(vmap()))/mul | solution.py:69
  235.9 40.8 %while.12 = (s32[]{:T(128)}, f32[32,8,577]{2,0,1:T(8,128)S(1)}, s32[4,3]{1,0:T(4,128)}, f32[4,32,5,513]{3,1,2,0:T(8,128)S(1)}, s32[]{:T(128)}, /*index=5*/s32[3]{0:T(128)S(1)}, s32[]{:T(128)}) while((s32[]{:T(128)}, f32[32,8,577]{2,0,1:T(8,128)S(1)}, s32[4,3]{1,0:T(4,128)}, f32[4,32,5,513]{3,1,2,0:T(8,128)S(1)}, s32[]{:T(128)}, ...), condition=%wide.while_cond.4, body=%wide.while_body.4.sunk | while | flops 164179 | bytes 3611691 | solution.py:63
  262.8 3.7 dynamic-update-slice.32
  273.0 3.7 dynamic-update-slice.32
  281.1 40.9 %while.13 = (s32[]{:T(128)}, f32[32,8,577]{2,0,1:T(8,128)S(1)}, s32[4,3]{1,0:T(4,128)}, f32[4,32,5,513]{3,1,2,0:T(8,128)S(1)}, s32[]{:T(128)}, /*index=5*/s32[3]{0:T(128)S(1)}, s32[]{:T(128)}) while((s32[]{:T(128)}, f32[32,8,577]{2,0,1:T(8,128)S(1)}, s32[4,3]{1,0:T(4,128)}, f32[4,32,5,513]{3,1,2,0:T(8,128)S(1)}, s32[]{:T(128)}, ...), condition=%wide.while_cond.5, body=%wide.while_body.5.sunk | while | flops 164179 | bytes 3611691 | solution.py:63
  297.9 3.7 dynamic-update-slice.33
  325.1 41.4 %while.14 = (s32[]{:T(128)}, f32[32,8,577]{2,0,1:T(8,128)S(1)}, s32[4,3]{1,0:T(4,128)}, f32[4,32,5,513]{3,1,2,0:T(8,128)S(1)}, s32[]{:T(128)}, /*index=5*/s32[3]{0:T(128)S(1)}, s32[]{:T(128)}) while((s32[]{:T(128)}, f32[32,8,577]{2,0,1:T(8,128)S(1)}, s32[4,3]{1,0:T(4,128)}, f32[4,32,5,513]{3,1,2,0:T(8,128)S(1)}, s32[]{:T(128)}, ...), condition=%wide.while_cond.6, body=%wide.while_body.6.sunk | while | flops 164179 | bytes 3611691 | solution.py:63
  352.3 3.7 dynamic-update-slice.34
  362.7 3.8 dynamic-update-slice.34
  369.9 41.3 %while.15 = (s32[]{:T(128)}, f32[32,8,577]{2,0,1:T(8,128)S(1)}, s32[4,3]{1,0:T(4,128)}, f32[4,32,5,513]{3,1,2,0:T(8,128)S(1)}, s32[]{:T(128)}, /*index=5*/s32[3]{0:T(128)S(1)}, s32[]{:T(128)}) while((s32[]{:T(128)}, f32[32,8,577]{2,0,1:T(8,128)S(1)}, s32[4,3]{1,0:T(4,128)}, f32[4,32,5,513]{3,1,2,0:T(8,128)S(1)}, s32[]{:T(128)}, ...), condition=%wide.while_cond.7, body=%wide.while_body.7.sunk | while | flops 164179 | bytes 3611691 | solution.py:63
  376.6 3.7 dynamic-update-slice.35
  411.9 89.3 %fusion.82 = f32[8,32,3,3,3]{1,0,4,3,2:T(8,128)S(1)} fusion(bf16[32,1,6,4,512]{0,1,4,3,2:T(2,128)(2,1)} %copy.203, bf16[8,1,4,4,512]{0,1,4,3,2:T(2,128)(2,1)} %copy.204), kind=kOutput, calls=%fused_computation.204 | convolution fusion | flops 94248960 | bytes 945152 | tf_op jit(solution)/shard_map/transpose | solution.py:87
  501.3 10.7 %copy.205 = bf16[8,1,6,4,512]{0,1,4,3,2:T(2,128)(2,1)} copy(bf16[8,1,6,4,512]{4,0,3,2,1:T(8,128)(2,1)S(1)} %maximum_bitcast_fusion.2) | data formatting | bytes 393216 | tf_op jit(solution)/shard_map/broadcast_in_dim | solution.py:80
  514.5 64.7 %fusion.83 = f32[8,8,3,3,3]{0,1,4,3,2:T(8,128)S(1)} fusion(bf16[8,1,6,4,512]{0,1,4,3,2:T(2,128)(2,1)} %copy.205, bf16[8,1,4,4,512]{0,1,4,3,2:T(2,128)(2,1)} %copy.206), kind=kOutput, calls=%fused_computation.205 | convolution fusion | flops 23562240 | bytes 334592 | tf_op jit(solution)/shard_map/transpose | solution.py:87
  579.2 44.3 %all-reduce.21 = (f32[8,32,3,3,3]{1,0,4,3,2:T(8,128)S(1)}, f32[8,8,3,3,3]{0,1,4,3,2:T(8,128)S(1)}) all-reduce(f32[8,32,3,3,3]{1,0,4,3,2:T(8,128)S(1)} %fusion.82, f32[8,8,3,3,3]{0,1,4,3,2:T(8,128)S(1)} %fusion.83), channel_id=1, replica_groups=mesh['cam'=16,'depth'=2] {'cam','depth'}, use_global_device_ids=true, to_apply=%region_7.8 | all-reduce | flops 8640 | bytes 69120 | tf_op jit(solution)/shard_map/psum | solution.py:167
  (402 shorter events, 291.2 us)
Async XLA Ops:
  7.2 153.8 %copy-start = (bf16[8,32,3,3,3]{1,0,4,3,2:T(8,128)(2,1)S(1)}, bf16[8,32,3,3,3]{1,0,4,3,2:T(8,128)(2,1)}, u32[]{:S(2)}) copy-start(bf16[8,32,3,3,3]{1,0,4,3,2:T(8,128)(2,1)} %param.16) | copy-start | bytes 41476
  7.2 28.4 %copy-start.11 = (bf16[1,8,4,4,512]{4,3,2,1,0:T(4,128)(2,1)S(1)}, bf16[1,8,4,4,512]{4,3,2,1,0:T(4,128)(2,1)}, u32[]{:S(2)}) copy-start(bf16[1,8,4,4,512]{4,3,2,1,0:T(4,128)(2,1)} %param.19) | copy-start | bytes 393220
  7.2 617.7 %reduce-scatter.2.cloned.1.call-start = ((), (), s32[]{:S(2)}) async-start(), calls=%async_computation.1 | async-start | bytes 786432 | tf_op jit(solution)/shard_map/reduce_scatter | solution.py:166
  9.0 48.2 %collective-permute-start.5 = (bf16[32,8,512]{2,0,1:T(8,128)(2,1)}, bf16[32,8,512]{2,0,1:T(8,128)(2,1)}, u32[]{:S(2)}, u32[]{:S(2)}) collective-permute-start(bf16[32,8,512]{2,0,1:T(8,128)(2,1)} %bitcast.243), channel_id=1, source_target_pairs={{0,28},{2,30},{4,0},{6,2},{8,4},{10,6},{12,8},{14,10},{16,12},{18,... | collective-permute-start | bytes 786440 | tf_op jit(solution)/shard_map/ppermute | solution.py:18
  15.0 55.6 %collective-permute-start.3 = (bf16[32,8,512]{2,0,1:T(8,128)(2,1)}, bf16[32,8,512]{2,0,1:T(8,128)(2,1)}, u32[]{:S(2)}, u32[]{:S(2)}) collective-permute-start(bf16[32,8,512]{2,0,1:T(8,128)(2,1)} %bitcast.243), channel_id=1, source_target_pairs={{0,2},{2,4},{4,6},{6,8},{8,10},{10,12},{12,14},{14,16},{16,18},{18... | collective-permute-start | bytes 786440 | tf_op jit(solution)/shard_map/ppermute | solution.py:18
  15.0 73.3 %collective-permute-start.2 = (bf16[32,8,512]{2,0,1:T(8,128)(2,1)}, bf16[32,8,512]{2,0,1:T(8,128)(2,1)}, u32[]{:S(2)}, u32[]{:S(2)}) collective-permute-start(bf16[32,8,512]{2,0,1:T(8,128)(2,1)} %bitcast.243), channel_id=1, source_target_pairs={{0,4},{2,6},{4,8},{6,10},{8,12},{10,14},{12,16},{14,18},{16,20},{1... | collective-permute-start | bytes 786440 | tf_op jit(solution)/shard_map/ppermute | solution.py:18
  15.8 30.4 %collective-permute-start = (bf16[8,1,4,512]{3,2,1,0:T(4,128)(2,1)S(1)}, bf16[8,1,4,512]{3,2,1,0:T(4,128)(2,1)S(1)}, u32[]{:S(2)}, u32[]{:S(2)}) collective-permute-start(bf16[8,1,4,512]{3,2,1,0:T(4,128)(2,1)S(1)} %get-tuple-element.368), channel_id=1, source_target_pairs={{0,1},{2,3},{4,5},{6,7},{8,9},{10,11},{12,13},{14,15},{16,17},{18,... | collective-permute-start | bytes 98312 | tf_op jit(solution)/shard_map/ppermute | solution.py:29
  19.2 31.2 %collective-permute-start.1 = (bf16[8,1,4,512]{3,2,1,0:T(4,128)(2,1)S(1)}, bf16[8,1,4,512]{3,2,1,0:T(4,128)(2,1)S(1)}, u32[]{:S(2)}, u32[]{:S(2)}) collective-permute-start(bf16[8,1,4,512]{3,2,1,0:T(4,128)(2,1)S(1)} %get-tuple-element.369), channel_id=1, source_target_pairs={{1,0},{3,2},{5,4},{7,6},{9,8},{11,10},{13,12},{15,14},{17,16},{19,... | collective-permute-start | bytes 98312 | tf_op jit(solution)/shard_map/ppermute | solution.py:31
  21.4 103.0 %copy-start.16 = (f32[4]{0:T(128)}, f32[4]{0:T(128)S(1)}, u32[]{:S(2)}) copy-start(f32[4]{0:T(128)S(1)} %get-tuple-element.376) | copy-start | bytes 52
  21.4 105.0 %copy-start.22 = (f32[4]{0:T(128)}, f32[4]{0:T(128)S(1)}, u32[]{:S(2)}) copy-start(f32[4]{0:T(128)S(1)} %get-tuple-element.377) | copy-start | bytes 52
  22.8 101.6 %copy-start.18 = (f32[4]{0:T(128)}, f32[4]{0:T(128)S(1)}, u32[]{:S(2)}) copy-start(f32[4]{0:T(128)S(1)} %get-tuple-element.379) | copy-start | bytes 52
  23.7 106.6 %copy-start.7 = (f32[32,4,512]{2,0,1:T(8,128)}, f32[32,4,512]{2,0,1:T(8,128)S(1)}, u32[]{:S(2)}) copy-start(f32[32,4,512]{2,0,1:T(8,128)S(1)} %slice_convert_fusion) | copy-start | bytes 786436
  26.8 103.6 %copy-start.20 = (f32[4]{0:T(128)}, f32[4]{0:T(128)S(1)}, u32[]{:S(2)}) copy-start(f32[4]{0:T(128)S(1)} %get-tuple-element.372) | copy-start | bytes 52
  46.2 60.0 %collective-permute-start.4 = (bf16[32,8,512]{2,0,1:T(8,128)(2,1)}, bf16[32,8,512]{2,0,1:T(8,128)(2,1)}, u32[]{:S(2)}, u32[]{:S(2)}) collective-permute-start(bf16[32,8,512]{2,0,1:T(8,128)(2,1)} %bitcast.243), channel_id=1, source_target_pairs={{0,30},{2,0},{4,2},{6,4},{8,6},{10,8},{12,10},{14,12},{16,14},{18,... | collective-permute-start | bytes 786440 | tf_op jit(solution)/shard_map/ppermute | solution.py:18
  130.4 12.1 %copy-start.6 = (bf16[8,6,4,1,8,65]{0,4,5,2,1,3:T(8,128)(2,1)S(1)}, bf16[8,6,4,1,8,65]{0,4,5,2,1,3:T(8,128)(2,1)}, u32[]{:S(2)}) copy-start(bf16[8,6,4,1,8,65]{0,4,5,2,1,3:T(8,128)(2,1)} %copy-done.5) | copy-start | bytes 599044
  130.4 12.1 %copy-start.15 = (bf16[8,6,4,1,7,2]{0,4,5,2,1,3:T(8,128)(2,1)S(1)}, bf16[8,6,4,1,7,2]{0,4,5,2,1,3:T(8,128)(2,1)}, u32[]{:S(2)}) copy-start(bf16[8,6,4,1,7,2]{0,4,5,2,1,3:T(8,128)(2,1)} %slice.380) | copy-start | bytes 16132
  130.4 12.1 %copy-start.38 = (bf16[8,8,3,3,3]{1,0,4,3,2:T(8,128)(2,1)S(1)}, bf16[8,8,3,3,3]{1,0,4,3,2:T(8,128)(2,1)}, u32[]{:S(2)}) copy-start(bf16[8,8,3,3,3]{1,0,4,3,2:T(8,128)(2,1)} %param.18) | copy-start | bytes 10372
  130.5 12.1 %copy-start.39 = (pred[8,65]{0,1:T(8,128)(4,1)S(1)}, pred[8,65]{0,1:T(8,128)(4,1)}, u32[]{:S(2)}) copy-start(pred[8,65]{0,1:T(8,128)(4,1)} %constant.234) | copy-start | bytes 1564
  136.6 17.5 %collective-permute-start.6 = (bf16[32,1,4,512]{3,0,2,1:T(8,128)(2,1)S(1)}, bf16[32,1,4,512]{3,0,2,1:T(8,128)(2,1)S(1)}, u32[]{:S(2)}, u32[]{:S(2)}) collective-permute-start(bf16[32,1,4,512]{3,0,2,1:T(8,128)(2,1)S(1)} %get-tuple-element.360), channel_id=1, source_target_pairs={{0,1},{2,3},{4,5},{6,7},{8,9},{10,11},{12,13},{14,15},{16,17},{18,... | collective-permute-start | bytes 393224 | tf_op jit(solution)/shard_map/ppermute | solution.py:29
  140.9 13.2 %collective-permute-start.7 = (bf16[32,1,4,512]{3,0,2,1:T(8,128)(2,1)S(1)}, bf16[32,1,4,512]{3,0,2,1:T(8,128)(2,1)S(1)}, u32[]{:S(2)}, u32[]{:S(2)}) collective-permute-start(bf16[32,1,4,512]{3,0,2,1:T(8,128)(2,1)S(1)} %get-tuple-element.361), channel_id=1, source_target_pairs={{1,0},{3,2},{5,4},{7,6},{9,8},{11,10},{13,12},{15,14},{17,16},{19,... | collective-permute-start | bytes 393224 | tf_op jit(solution)/shard_map/ppermute | solution.py:31
  175.5 20.3 %copy-start.12 = (bf16[8,4,4,512]{3,0,2,1:T(8,128)(2,1)}, bf16[8,4,4,512]{3,0,2,1:T(8,128)(2,1)S(1)}, u32[]{:S(2)}) copy-start(bf16[8,4,4,512]{3,0,2,1:T(8,128)(2,1)S(1)} %get-tuple-element.362) | copy-start | bytes 393220
  175.7 30.8 %collective-permute-start.8 = (bf16[8,1,4,512]{3,0,2,1:T(8,128)(2,1)S(1)}, bf16[8,1,4,512]{3,0,2,1:T(8,128)(2,1)S(1)}, u32[]{:S(2)}, u32[]{:S(2)}) collective-permute-start(bf16[8,1,4,512]{3,0,2,1:T(8,128)(2,1)S(1)} %get-tuple-element.366), channel_id=1, source_target_pairs={{0,1},{2,3},{4,5},{6,7},{8,9},{10,11},{12,13},{14,15},{16,17},{18,... | collective-permute-start | bytes 98312 | tf_op jit(solution)/shard_map/ppermute | solution.py:29
  180.2 26.2 %collective-permute-start.9 = (bf16[8,1,4,512]{3,0,2,1:T(8,128)(2,1)S(1)}, bf16[8,1,4,512]{3,0,2,1:T(8,128)(2,1)S(1)}, u32[]{:S(2)}, u32[]{:S(2)}) collective-permute-start(bf16[8,1,4,512]{3,0,2,1:T(8,128)(2,1)S(1)} %get-tuple-element.367), channel_id=1, source_target_pairs={{1,0},{3,2},{5,4},{7,6},{9,8},{11,10},{13,12},{15,14},{17,16},{19,... | collective-permute-start | bytes 98312 | tf_op jit(solution)/shard_map/ppermute | solution.py:31
  182.2 229.3 %collective-permute-start.14 = (bf16[8,1,4,512]{3,0,2,1:T(8,128)(2,1)}, bf16[8,1,4,512]{3,0,2,1:T(8,128)(2,1)S(1)}, u32[]{:S(2)}, u32[]{:S(2)}) collective-permute-start(bf16[8,1,4,512]{3,0,2,1:T(8,128)(2,1)} %get-tuple-element.364), channel_id=1, source_target_pairs={{0,1},{2,3},{4,5},{6,7},{8,9},{10,11},{12,13},{14,15},{16,17},{18,... | collective-permute-start | bytes 98312 | tf_op jit(solution)/shard_map/ppermute | solution.py:29
  186.7 314.5 %collective-permute-start.15 = (bf16[8,1,4,512]{3,0,2,1:T(8,128)(2,1)}, bf16[8,1,4,512]{3,0,2,1:T(8,128)(2,1)S(1)}, u32[]{:S(2)}, u32[]{:S(2)}) collective-permute-start(bf16[8,1,4,512]{3,0,2,1:T(8,128)(2,1)} %get-tuple-element.365), channel_id=1, source_target_pairs={{1,0},{3,2},{5,4},{7,6},{9,8},{11,10},{13,12},{15,14},{17,16},{19,... | collective-permute-start | bytes 98312 | tf_op jit(solution)/shard_map/ppermute | solution.py:31
  235.9 43.0 %copy-start.21 = (f32[4]{0:T(128)S(1)}, f32[4]{0:T(128)}, u32[]{:S(2)}) copy-start(f32[4]{0:T(128)} %copy-done.20) | copy-start | bytes 52
  277.0 235.0 %collective-permute-start.10 = (f32[32,8,512]{2,0,1:T(8,128)S(1)}, f32[32,8,512]{2,0,1:T(8,128)}, u32[]{:S(2)}, u32[]{:S(2)}) collective-permute-start(f32[32,8,512]{2,0,1:T(8,128)S(1)} %slice.234), channel_id=1, source_target_pairs={{0,28},{2,30},{4,0},{6,2},{8,4},{10,6},{12,8},{14,10},{16,12},{18,... | collective-permute-start | bytes 1572872 | tf_op jit(solution)/shard_map/ppermute | solution.py:18
  323.0 189.0 %collective-permute-start.11 = (f32[32,8,512]{2,0,1:T(8,128)}, f32[32,8,512]{2,0,1:T(8,128)}, u32[]{:S(2)}, u32[]{:S(2)}) collective-permute-start(f32[32,8,512]{2,0,1:T(8,128)} %slice.235), channel_id=1, source_target_pairs={{0,30},{2,0},{4,2},{6,4},{8,6},{10,8},{12,10},{14,12},{16,14},{18,... | collective-permute-start | bytes 1572872 | tf_op jit(solution)/shard_map/ppermute | solution.py:18
  367.5 144.5 %collective-permute-start.12 = (f32[32,8,512]{2,0,1:T(8,128)}, f32[32,8,512]{2,0,1:T(8,128)}, u32[]{:S(2)}, u32[]{:S(2)}) collective-permute-start(f32[32,8,512]{2,0,1:T(8,128)} %slice.236), channel_id=1, source_target_pairs={{0,2},{2,4},{4,6},{6,8},{8,10},{10,12},{12,14},{14,16},{16,18},{18... | collective-permute-start | bytes 1572872 | tf_op jit(solution)/shard_map/ppermute | solution.py:18
  411.5 89.7 %copy-start.13 = (bf16[8,4,4,512]{3,0,2,1:T(8,128)(2,1)S(1)}, bf16[8,4,4,512]{3,0,2,1:T(8,128)(2,1)}, u32[]{:S(2)}) copy-start(bf16[8,4,4,512]{3,0,2,1:T(8,128)(2,1)} %copy-done.12) | copy-start | bytes 393220
  411.5 100.5 %collective-permute-start.13 = (f32[32,8,512]{2,0,1:T(8,128)S(1)}, f32[32,8,512]{2,0,1:T(8,128)S(1)}, u32[]{:S(2)}, u32[]{:S(2)}) collective-permute-start(f32[32,8,512]{2,0,1:T(8,128)S(1)} %slice.237), channel_id=1, source_target_pairs={{0,4},{2,6},{4,8},{6,10},{8,12},{10,14},{12,16},{14,18},{16,20},{1... | collective-permute-start | bytes 1572872 | tf_op jit(solution)/shard_map/ppermute | solution.py:18
  514.5 112.2 %copy-start.1 = (bf16[8,32,3,3,3]{1,0,4,3,2:T(8,128)(2,1)S(1)}, bf16[8,32,3,3,3]{1,0,4,3,2:T(8,128)(2,1)}, u32[]{:S(2)}) copy-start(bf16[8,32,3,3,3]{1,0,4,3,2:T(8,128)(2,1)} %param.16) | copy-start | bytes 41476
  (26 other events, 71.5 us)
Sparse Core Ops, SparseCore 0:
  514.6 17.2 reduce-scatter.1
where the time goes:
time: 643 us; the launch traced here: 634 us
  local copies, waits for them, and re-layouts  252 us (39%)
  matrix products  180 us (28%)
  other arithmetic  105 us (16%)
  blocking collectives  44.3 us (7%)
  starting transfers between devices  35.1 us (5%)
  between operations  15.9 us (2%)
    transpose x2, matrix products, weight_term(): return jnp.transpose(result, (1, 0, 2, 3, 4))  154 us
    scatter-add x96, local copies, waits for them, and re-layouts  104 us
    scatter-add x32, other arithmetic  59.3 us
    gather x80, local copies, waits for them, and re-layouts  57.7 us
    psum x1, blocking collectives, shards(): lax.psum((first_term, second_term), ('cam', 'depth'))  44.3 us
    conv_general_dilated x14, local copies, waits for them, and re-layouts, conv_same(): lax.conv_general_dilated(volume[None], kernel, (1, 1, 1), [depth_pad, (1,...  27.5 us
    conv_general_dilated x3, matrix products, conv_same(): lax.conv_general_dilated(volume[None], kernel, (1, 1, 1), [depth_pad, (1,...  25.7 us
    broadcast_in_dim x2, local copies, waits for them, and re-layouts, weight_term(): volume[:, None]  21.4 us
  transfers between devices with their start and end apart: 17, of which 0 were waited for; matrix products, arithmetic and copies ran while one was open for 75% of the time, Pallas kernels for 0%

commit v1 on v0

v1 whole, which is shorter than its diff:
```python
import functools

import jax
import jax.numpy as jnp
from jax import lax
from jax.experimental import pallas as pl
from jax.experimental.pallas import tpu as pltpu
from jax.sharding import PartitionSpec as P

SHIFT = 32
view_offsets = (-2, -1, 1, 2)
SMEM = pl.BlockSpec(memory_space=pltpu.SMEM)
VMEM = pl.BlockSpec(memory_space=pltpu.VMEM)


def banded(kernel, height):
    taps = jnp.transpose(kernel, (4, 0, 2, 3, 1))
    zero = jnp.zeros((), kernel.dtype)
    rows = []
    for h in range(height):
        rows.append(lax.pad(taps, zero, [(0, 0, 0)] * 3 + [(h - 1, height - 2 - h, 0)] + [(0, 0, 0)]))
    return jnp.stack(rows, axis=1)


def flipped(kernel):
    return jnp.transpose(jnp.flip(kernel, (2, 3, 4)), (1, 0, 2, 3, 4))


def mul(a, b):
    return jnp.dot(a, b, preferred_element_type=jnp.float32)


def mul_t(a, b):
    return lax.dot_general(a, b, (((1,), (1,)), ((), ())), preferred_element_type=jnp.float32)


def lanes(width):
    return lax.broadcasted_iota(jnp.int32, (1, width), 1)


def from_left(x):
    width = x.shape[1]
    return jnp.where(lanes(width) > 0, pltpu.roll(x, 1, 1), 0.0)


def from_right(x):
    width = x.shape[1]
    return jnp.where(lanes(width) < width - 1, pltpu.roll(x, width - 1, 1), 0.0)


def compute(
    dims,
    row_ref, col_ref, fy_ref, fx_ref, m_ref, inv_ref,
    feat_ref, cot_ref, b1_ref, b2_ref, b3_ref, bias_ref,
    grad_ref, wsum_ref,
    warp, mean, cost, scot, spre, pre_acc, hid, acc1, acc2, cg,
):
    chans, mid, height, width, own, planes, top = dims
    band = height * chans
    mband = height * mid
    first_own = (planes - own) * lax.axis_index("depth")
    inv = inv_ref[0]

    def weights(s, p):
        c = col_ref[s, p]
        fx = fx_ref[s, p]
        at = lanes(width) + c
        left = jnp.where((at >= 0) & (at < width), 1.0 - fx, 0.0)
        right = jnp.where((at >= -1) & (at < width - 1), fx, 0.0)
        return c, left, right

    for end in (0, planes + 1):
        scot[end * 3 * mband : (end + 1) * 3 * mband, :] = jnp.zeros((3 * mband, width), scot.dtype)
        spre[end * 3 * mband : (end + 1) * 3 * mband, :] = jnp.zeros((3 * mband, width), spre.dtype)
        cost[end * band : (end + 1) * band, :] = jnp.zeros((band, width), cost.dtype)
    for p in range(planes):
        plane = cot_ref[p * mband : (p + 1) * mband, :]
        wide = plane.astype(jnp.float32)
        base = (p + 1) * 3 * mband
        scot[base : base + mband, :] = from_left(wide).astype(scot.dtype)
        scot[base + mband : base + 2 * mband, :] = plane
        scot[base + 2 * mband : base + 3 * mband, :] = from_right(wide).astype(scot.dtype)

    def warp_plane(p, _):
        for h in range(height):
            ref = feat_ref[0, (top + h) * chans : (top + h + 1) * chans, :].astype(jnp.float32)
            first = ref
            second = ref * ref
            for s in range(4):
                c, left, right = weights(s, p)
                fy = fy_ref[s, p]
                start = pl.multiple_of((row_ref[s, p] + h) * chans, chans)
                upper = feat_ref[s + 1, pl.ds(start, chans), :].astype(jnp.float32)
                start = pl.multiple_of((row_ref[s, p] + h + 1) * chans, chans)
                lower = feat_ref[s + 1, pl.ds(start, chans), :].astype(jnp.float32)
                mixed = (1.0 - fy) * upper + fy * lower
                here = pltpu.roll(mixed, jnp.where(c > 0, width - c, -c), 1)
                after = pltpu.roll(here, width - 1, 1)
                warped = left * here + right * after
                warp[s, p, h * chans : (h + 1) * chans, :] = warped
                weighted = m_ref[s] * warped
                first = first + weighted
                second = second + weighted * warped
            average = first * inv
            mean[p, h * chans : (h + 1) * chans, :] = average
            at = pl.multiple_of((p + 1) * band + h * chans, chans)
            cost[pl.ds(at, chans), :] = (second * inv - average * average).astype(cost.dtype)
        return 0

    lax.fori_loop(0, planes, warp_plane, 0)

    def middle(i, _):
        p = first_own // 2 + i
        x = cost[pl.ds(pl.multiple_of(p * band, band), 3 * band), :]
        parts = mul(b1_ref[...], x)
        pre = from_left(parts[:mband]) + parts[mband : 2 * mband] + from_right(parts[2 * mband :])
        pre = pre + bias_ref[...]
        gate = jax.nn.sigmoid(pre)
        hid[pl.ds(pl.multiple_of(p * mband, mband), mband), :] = (pre * gate).astype(hid.dtype)
        y = scot[pl.ds(pl.multiple_of(p * 3 * mband, 3 * mband), 3 * 3 * mband), :]
        back = mul(b2_ref[...], y) * (gate * (1.0 + pre * (1.0 - gate)))
        base = pl.multiple_of((p + 1) * 3 * mband, mband)
        spre[pl.ds(base, mband), :] = from_left(back).astype(spre.dtype)
        spre[pl.ds(base + mband, mband), :] = back.astype(spre.dtype)
        spre[pl.ds(base + 2 * mband, mband), :] = from_right(back).astype(spre.dtype)
        return 0

    lax.fori_loop(0, own + (planes - own) // 2, middle, 0)

    grad_ref[...] = jnp.zeros_like(grad_ref)
    acc1[...] = jnp.zeros_like(acc1)
    acc2[...] = jnp.zeros_like(acc2)

    def back_plane(i, _):
        p = first_own + i
        s3 = spre[pl.ds(pl.multiple_of(p * 3 * mband, 3 * mband), 9 * mband), :]
        c3 = scot[pl.ds(pl.multiple_of(p * 3 * mband, 3 * mband), 9 * mband), :]
        cg[...] = mul(b3_ref[...], s3) * (2.0 * inv)
        acc1[...] += mul_t(s3, cost[pl.ds(pl.multiple_of((p + 1) * band, band), band), :])
        acc2[:, :mband] += mul_t(c3, hid[pl.ds(pl.multiple_of(p * mband, mband), mband), :])
        for h in range(height):
            rows = slice(h * chans, (h + 1) * chans)
            ref = feat_ref[0, (top + h) * chans : (top + h + 1) * chans, :].astype(jnp.float32)
            grad_ref[0, (top + h) * chans : (top + h + 1) * chans, :] += cg[rows, :] * (ref - mean[p, rows, :])
        for s in range(4):
            c, left, right = weights(s, p)
            fy = fy_ref[s, p]
            turn = jnp.where(c < 0, width + c, c)
            carried = None
            for h in range(height + 1):
                if h < height:
                    rows = slice(h * chans, (h + 1) * chans)
                    grad = (m_ref[s] * cg[rows, :]) * (warp[s, p, rows, :] - mean[p, rows, :])
                    spread = pltpu.roll(left * grad + pltpu.roll(right * grad, 1, 1), turn, 1)
                    value = (1.0 - fy) * spread
                    if carried is not None:
                        value = value + carried
                    carried = fy * spread
                else:
                    value = carried
                start = pl.multiple_of((row_ref[s, p] + h) * chans, chans)
                grad_ref[s + 1, pl.ds(start, chans), :] += value
        return 0

    lax.fori_loop(0, own, back_plane, 0)

    def fold(acc, block, offset):
        rows = acc[...].reshape(9, height, mid, 128)
        lane = lax.broadcasted_iota(jnp.int32, (1, 1, 128), 2)
        total = None
        for g in range(height):
            ok = (lane >= (g - 1) * block) & (lane < (g + 2) * block) & (lane < height * block)
            part = jnp.where(ok, rows[:, g], 0.0).reshape(9 * mid, 128)
            turn = (offset - (g - 1) * block) % 128
            if turn:
                part = pltpu.roll(part, turn, 1)
            total = part if total is None else total + part
        return total

    wsum_ref[...] = fold(acc1, chans, 0) + fold(acc2, mid, 3 * chans)


def shards(
    features, view_mask, row_offset, frac_row, col_offset, frac_col,
    first_kernel, first_bias, second_kernel, cotangent,
):
    cams, slabs = lax.axis_size("cam"), lax.axis_size("depth")
    _, chans, held, width = features.shape
    mid = first_kernel.shape[0]
    _, _, own, height, _ = cotangent.shape
    top = (held - height) // 2
    band, mband = height * chans, height * mid
    assert slabs == 2 and own >= 2 and band == 128
    planes = own + 2
    me = lax.axis_index("depth")
    swap = [(0, 1), (1, 0)]

    own_band = jnp.transpose(features[0], (1, 0, 2)).reshape(held * chans, width)
    bands = [own_band]
    for offset in view_offsets:
        bands.append(lax.ppermute(own_band, "cam", [((i + offset) % cams, i) for i in range(cams)]))
    feat = jnp.stack(bands)

    def widened(x, axis):
        edge = lax.dynamic_slice_in_dim(x, (own - 2) * (1 - me), 2, axis)
        other = lax.ppermute(edge, "depth", swap)
        return jnp.where(
            me == 0, jnp.concatenate([x, other], axis), jnp.concatenate([other, x], axis)
        )

    cot = jnp.transpose(cotangent[0], (1, 2, 0, 3)).reshape(own, mband, width)
    cot = widened(cot, 0).reshape(planes * mband, width)
    scalars = jnp.stack(
        [row_offset[0].astype(jnp.float32), col_offset[0].astype(jnp.float32), frac_row[0], frac_col[0]]
    )
    scalars = widened(scalars, 2)
    mask = view_mask[0].astype(jnp.float32)
    inv = (1.0 / (1.0 + jnp.sum(mask))).reshape(1)

    b1 = banded(first_kernel, height).reshape(3 * mband, 3 * band)
    b2 = jnp.transpose(banded(flipped(second_kernel), height), (1, 2, 3, 0, 4, 5)).reshape(mband, 9 * mband)
    b3 = jnp.transpose(banded(flipped(first_kernel), height), (1, 2, 3, 0, 4, 5)).reshape(band, 9 * mband)
    bias = jnp.tile(first_bias, height).reshape(mband, 1)

    f32, bf16 = jnp.float32, jnp.bfloat16
    grads, wsum = pl.pallas_call(
        functools.partial(compute, (chans, mid, height, width, own, planes, top)),
        out_shape=(
            jax.ShapeDtypeStruct((5, held * chans, width), f32),
            jax.ShapeDtypeStruct((9 * mid, 128), f32),
        ),
        in_specs=[SMEM] * 6 + [VMEM] * 6,
        out_specs=(VMEM, VMEM),
        scratch_shapes=[
            pltpu.VMEM((4, planes, band, width), f32),
            pltpu.VMEM((planes, band, width), f32),
            pltpu.VMEM(((planes + 2) * band, width), bf16),
            pltpu.VMEM(((planes + 2) * 3 * mband, width), bf16),
            pltpu.VMEM(((planes + 2) * 3 * mband, width), bf16),
            pltpu.VMEM((8, 128), f32),
            pltpu.VMEM((planes * mband, width), bf16),
            pltpu.VMEM((9 * mband, 128), f32),
            pltpu.VMEM((9 * mband, 128), f32),
            pltpu.VMEM((band, width), f32),
        ],
        compiler_params=pltpu.CompilerParams(vmem_limit_bytes=40 * 2**20),
        name="core",
    )(
        scalars[0].astype(jnp.int32), scalars[1].astype(jnp.int32), scalars[2], scalars[3], mask, inv,
        feat, cot, b1, b2, b3, bias,
    )

    grads = grads.reshape(5, held, chans, width)
    part = lax.psum_scatter(grads, "depth", scatter_dimension=2, tiled=True)
    summed = part[0]
    for s, offset in enumerate(view_offsets):
        summed = summed + lax.ppermute(part[s + 1], "cam", [(i, (i + offset) % cams) for i in range(cams)])
    feature_grad = jnp.transpose(summed, (1, 0, 2))
    wsum = lax.psum(wsum, ("cam", "depth"))
    scale = (cams * slabs * own * height * width) ** (-0.5)
    taps = (wsum * scale).reshape(3, 3, mid, 128)[::-1, ::-1]
    first = taps[..., : 3 * chans].reshape(3, 3, mid, 3, chans)
    second = taps[..., 3 * chans : 3 * chans + 3 * mid].reshape(3, 3, mid, 3, mid)
    order = (2, 4, 0, 3, 1)
    return feature_grad[None], jnp.transpose(first, order), jnp.transpose(second, order)


def solution(mesh):
    placed = (
        P("cam", None, None, None),
        P("cam", None),
        P("cam", None, "depth"),
        P("cam", None, "depth"),
        P("cam", None, "depth"),
        P("cam", None, "depth"),
        P(),
        P(),
        P(),
        P("cam", None, "depth", None, None),
    )
    return jax.shard_map(
        shards,
        mesh=mesh,
        in_specs=placed,
        out_specs=(P("cam", "depth", None, None), P(), P()),
        check_vma=False,
    )
```

time: 643 us -> 154 us (0.24); the launches traced: 634 us -> 154 us
  local copies, waits for them, and re-layouts: 252 us -> 12 us
  matrix products: 180 us -> 0 us
  other arithmetic: 105 us -> 5.26 us
  waiting for transfers between devices: 0.06 us -> 41.6 us
  starting transfers between devices: 35.1 us -> 18.1 us
  Pallas kernels: 0 us -> 16.9 us
    transpose x2 -> x0, matrix products: 154 us -> none  [weight_term(): return jnp.transpose(result, (1, 0, 2, 3, 4))]
    scatter-add x96 -> x0, local copies, waits for them, and re-layouts: 104 us -> none
    scatter-add x32 -> x0, other arithmetic: 59.3 us -> none
    gather x80 -> x0, local copies, waits for them, and re-layouts: 57.7 us -> none
    unnamed x1 -> x2, waiting for transfers between devices: 0.02 us -> 37.9 us
    conv_general_dilated x14 -> x0, local copies, waits for them, and re-layouts: 27.5 us -> none  [conv_same(): lax.conv_general_dilated(volume[None], kernel, (1, 1, 1), [depth_pad, (1,...]
    conv_general_dilated x3 -> x0, matrix products: 25.7 us -> none  [conv_same(): lax.conv_general_dilated(volume[None], kernel, (1, 1, 1), [depth_pad, (1,...]
    broadcast_in_dim x5 -> x0, local copies, waits for them, and re-layouts: 22.3 us -> none  [the longest x2 21.4 us: weight_term(): volume[:, None]]
  transfers between devices with their start and end apart: 17 -> 11, of which waited for: 0 -> 2; matrix products, arithmetic and copies ran while one was open for 75% -> 7% of each run, Pallas kernels for 0% -> 0%
where the time goes in v1:
time: 154 us
  blocking collectives  45 us (29%)
  waiting for transfers between devices  41.6 us (27%)
  starting transfers between devices  18.1 us (12%)
  Pallas kernels  16.9 us (11%)
  between operations  15 us (10%)
  local copies, waits for them, and re-layouts  12 us (8%)
  other arithmetic  5.26 us (3%)
    psum x1, blocking collectives, shards(): wsum = lax.psum(wsum, ('cam', 'depth'))  45 us
    unnamed x2, waiting for transfers between devices  37.9 us
    pallas_call x1, Pallas kernels, shards(): pl.pallas_call(functools.partial(compute, (chans, mid, height, width, own...  16.9 us
    ppermute x4, starting transfers between devices, shards(): lax.ppermute(part[s + 1], 'cam', [(i, (i + offset) % cams) for i in range...  8.69 us
    ppermute x4, starting transfers between devices, shards(): lax.ppermute(own_band, 'cam', [((i + offset) % cams, i) for i in range(ca...  7.25 us
    unnamed x15, local copies, waits for them, and re-layouts  6.21 us
    ppermute x2, waiting for transfers between devices, widened(): other = lax.ppermute(edge, 'depth', swap)  3.67 us
  transfers between devices with their start and end apart: 11, of which 2 were waited for; matrix products, arithmetic and copies ran while one was open for 7% of the time, Pallas kernels for 0%

profile of v1, /device:TPU:0, one launch (start us, length us, event | category | flops | bytes accessed | tf_op | source)
XLA Modules:
  0.0 153.8 jit_solution(11865083616188725292)
XLA Ops:
  7.2 1.0 copy.31
  8.2 6.0 %collective-permute-start.4 = (bf16[256,512]{1,0:T(8,128)(2,1)S(1)}, bf16[256,512]{1,0:T(8,128)(2,1)S(1)}, u32[]{:S(2)}, u32[]{:S(2)}) collective-permute-start(bf16[256,512]{1,0:T(8,128)(2,1)S(1)} %bitcast.132), channel_id=1, source_target_pairs={{4,0},{6,2},{8,4},{10,6},{12,8},{14,10},{16,12},{18,14},{20,16},{2... | collective-permute-start | bytes 786440 | tf_op jit(solution)/shard_map/ppermute | solution.py:201
  14.3 0.5 collective-permute-start.2
  14.8 0.7 collective-permute-start.1
  15.5 0.7 convert_element_type.23
  16.2 0.7 convert_element_type.24
  16.9 0.8 dynamic-slice_maximum_fusion
  17.6 1.5 collective-permute-start
  19.2 1.3 convert_reduce_fusion
  20.4 0.7 convert_bitcast_fusion.m_ref
  21.8 0.7 tile.2
  22.5 0.8 reverse_bitcast_fusion.1
  23.3 0.8 reverse_bitcast_fusion
  24.2 1.0 copy.54
  25.3 0.2 copy.36
  25.5 0.2 reshape.50
  25.9 0.2 copy.35
  26.2 0.2 reshape.49.b2_ref
  26.7 0.2 reshape.48.b1_ref
  26.9 0.6 collective-permute-start.5
  27.5 3.7 %collective-permute-done.5 = bf16[2,32,512]{2,1,0:T(8,128)(2,1)S(1)} collective-permute-done((bf16[2,32,512]{2,1,0:T(8,128)(2,1)S(1)}, bf16[2,32,512]{2,1,0:T(8,128)(2,1)S(1)}, u32[]{:S(2)}, u32[]{:S(2)}) %collective-permute-start.5) | collective-permute-done | bytes 65568 | tf_op jit(solution)/shard_map/ppermute | solution.py:206
  31.4 16.9 %core.1 = (f32[5,256,512]{2,1,0:T(8,128)S(1)}, f32[72,128]{1,0:T(8,128)S(1)}) custom-call(s32[4,6]{1,0:T(4,128)S(1)} %get-tuple-element.32.row_ref, s32[4,6]{1,0:T(4,128)S(1)} %get-tuple-element.31.col_ref, f32[4,6]{1,0:T(4,128)S(1)} %get-tuple-element.30.fy_ref, f32[4,6]{1,0:T(4,128)S(1)} %get-tuple-element.29.fx_ref, f32[4]{0:T(128)S(1)} %convert_bitcast_fusion.m_ref, ...), custom_call_target="tpu_custom_call" | custom-call | tf_op jit(solution)/shard_map/core/pallas_call | solution.py:226
  48.3 1.7 %copy.50 = f32[4,8,40,512]{3,1,2,0:T(8,128)} copy(f32[4,8,40,512]{3,1,0,2:T(8,128)S(1)} %bitcast.126) | data formatting | bytes 5242880
  50.1 37.9 %reduce-scatter.5.cloned.1.call-done = f32[16,20480]{1,0:T(8,128)} async-done(((f32[32,20480]{1,0:T(8,128)}), f32[16,20480]{1,0:T(8,128)}) %reduce-scatter.5.cloned.1.call-update) | async-done | bytes 1310736
  87.9 2.1 %copy.51 = f32[2,8,40,512]{3,2,1,0:T(8,128)S(1)} copy(f32[2,8,40,512]{3,1,2,0:T(8,128)} %bitcast.131) | data formatting | bytes 2621440
  90.0 0.8 slice_bitcast_fusion.3
  90.8 4.2 %collective-permute-start.6 = (f32[8,16,512]{2,0,1:T(8,128)}, f32[8,16,512]{2,0,1:T(8,128)S(1)}, u32[]{:S(2)}, u32[]{:S(2)}) collective-permute-start(f32[8,16,512]{2,0,1:T(8,128)} %get-tuple-element.13), channel_id=1, source_target_pairs={{0,28},{2,30},{4,0},{6,2},{8,4},{10,6},{12,8},{14,10},{16,12},{18,... | collective-permute-start | bytes 786440 | tf_op jit(solution)/shard_map/ppermute | solution.py:257
  95.1 4.4 %collective-permute-start.7 = (f32[8,16,512]{2,0,1:T(8,128)S(1)}, f32[8,16,512]{2,0,1:T(8,128)S(1)}, u32[]{:S(2)}, u32[]{:S(2)}) collective-permute-start(f32[8,16,512]{2,0,1:T(8,128)S(1)} %get-tuple-element.15), channel_id=1, source_target_pairs={{0,30},{2,0},{4,2},{6,4},{8,6},{10,8},{12,10},{14,12},{16,14},{18,... | collective-permute-start | bytes 786440 | tf_op jit(solution)/shard_map/ppermute | solution.py:257
  99.5 45.0 %psum.7 = f32[72,128]{1,0:T(8,128)S(1)} all-reduce(f32[72,128]{1,0:T(8,128)S(1)} %get-tuple-element.6), channel_id=1, replica_groups=mesh['cam'=16,'depth'=2] {'cam','depth'}, use_global_device_ids=true, to_apply=%region_2.3 | all-reduce | flops 9216 | bytes 73728 | tf_op jit(solution)/shard_map/psum | solution.py:259
  144.7 0.7 copy.41
  145.5 0.7 copy.40
  146.2 0.8 fusion.4
  (44 shorter events, 1.3 us)
Async XLA Ops:
  7.2 80.8 %reduce-scatter.5.cloned.1.call-start = ((), (), s32[]{:S(2)}) async-start(), calls=%async_computation.1 | async-start | bytes 3932160
  8.2 23.1 %collective-permute-start.4 = (bf16[256,512]{1,0:T(8,128)(2,1)S(1)}, bf16[256,512]{1,0:T(8,128)(2,1)S(1)}, u32[]{:S(2)}, u32[]{:S(2)}) collective-permute-start(bf16[256,512]{1,0:T(8,128)(2,1)S(1)} %bitcast.132), channel_id=1, source_target_pairs={{4,0},{6,2},{8,4},{10,6},{12,8},{14,10},{16,12},{18,14},{20,16},{2... | collective-permute-start | bytes 786440 | tf_op jit(solution)/shard_map/ppermute | solution.py:201
  14.3 17.0 %collective-permute-start.3 = (bf16[256,512]{1,0:T(8,128)(2,1)S(1)}, bf16[256,512]{1,0:T(8,128)(2,1)S(1)}, u32[]{:S(2)}, u32[]{:S(2)}) collective-permute-start(bf16[256,512]{1,0:T(8,128)(2,1)S(1)} %bitcast.133), channel_id=1, source_target_pairs={{2,0},{4,2},{6,4},{8,6},{10,8},{12,10},{14,12},{16,14},{18,16},{20... | collective-permute-start | bytes 786440 | tf_op jit(solution)/shard_map/ppermute | solution.py:201
  14.3 17.0 %collective-permute-start.2 = (bf16[256,512]{1,0:T(8,128)(2,1)S(1)}, bf16[256,512]{1,0:T(8,128)(2,1)S(1)}, u32[]{:S(2)}, u32[]{:S(2)}) collective-permute-start(bf16[256,512]{1,0:T(8,128)(2,1)S(1)} %bitcast.134), channel_id=1, source_target_pairs={{30,0},{0,2},{2,4},{4,6},{6,8},{8,10},{10,12},{12,14},{14,16},{16,... | collective-permute-start | bytes 786440 | tf_op jit(solution)/shard_map/ppermute | solution.py:201
  14.8 16.5 %collective-permute-start.1 = (bf16[256,512]{1,0:T(8,128)(2,1)S(1)}, bf16[256,512]{1,0:T(8,128)(2,1)S(1)}, u32[]{:S(2)}, u32[]{:S(2)}) collective-permute-start(bf16[256,512]{1,0:T(8,128)(2,1)S(1)} %bitcast.135), channel_id=1, source_target_pairs={{28,0},{30,2},{0,4},{2,6},{4,8},{6,10},{8,12},{10,14},{12,16},{14,... | collective-permute-start | bytes 786440 | tf_op jit(solution)/shard_map/ppermute | solution.py:201
  17.6 9.2 %collective-permute-start = (f32[4,4,2]{2,1,0:T(4,128)S(1)}, f32[4,4,2]{2,1,0:T(4,128)S(1)}, u32[]{:S(2)}, u32[]{:S(2)}) collective-permute-start(f32[4,4,2]{2,1,0:T(4,128)S(1)} %dynamic-slice_maximum_fusion), channel_id=1, source_target_pairs={{0,1},{1,0},{2,3},{3,2},{4,5},{5,4},{6,7},{7,6},{8,9},{9,8},{10,11... | collective-permute-start | bytes 392 | tf_op jit(solution)/shard_map/ppermute | solution.py:206
  25.5 0.9 copy-start
  26.1 1.3 copy-start.1
  26.2 1.3 copy-start.2
  26.9 4.3 %collective-permute-start.5 = (bf16[2,32,512]{2,1,0:T(8,128)(2,1)S(1)}, bf16[2,32,512]{2,1,0:T(8,128)(2,1)S(1)}, u32[]{:S(2)}, u32[]{:S(2)}) collective-permute-start(bf16[2,32,512]{2,1,0:T(8,128)(2,1)S(1)} %constant_dynamic-slice_fusion), channel_id=1, source_target_pairs={{0,1},{1,0},{2,3},{3,2},{4,5},{5,4},{6,7},{7,6},{8,9},{9,8},{10,11... | collective-permute-start | bytes 196616 | tf_op jit(solution)/shard_map/ppermute | solution.py:206
  90.8 55.3 %collective-permute-start.6 = (f32[8,16,512]{2,0,1:T(8,128)}, f32[8,16,512]{2,0,1:T(8,128)S(1)}, u32[]{:S(2)}, u32[]{:S(2)}) collective-permute-start(f32[8,16,512]{2,0,1:T(8,128)} %get-tuple-element.13), channel_id=1, source_target_pairs={{0,28},{2,30},{4,0},{6,2},{8,4},{10,6},{12,8},{14,10},{16,12},{18,... | collective-permute-start | bytes 786440 | tf_op jit(solution)/shard_map/ppermute | solution.py:257
  95.0 51.1 %collective-permute-start.8 = (f32[8,16,512]{2,0,1:T(8,128)S(1)}, f32[8,16,512]{2,0,1:T(8,128)S(1)}, u32[]{:S(2)}, u32[]{:S(2)}) collective-permute-start(f32[8,16,512]{2,0,1:T(8,128)S(1)} %get-tuple-element.14), channel_id=1, source_target_pairs={{0,2},{2,4},{4,6},{6,8},{8,10},{10,12},{12,14},{14,16},{16,18},{18... | collective-permute-start | bytes 786440 | tf_op jit(solution)/shard_map/ppermute | solution.py:257
  95.1 51.1 %collective-permute-start.7 = (f32[8,16,512]{2,0,1:T(8,128)S(1)}, f32[8,16,512]{2,0,1:T(8,128)S(1)}, u32[]{:S(2)}, u32[]{:S(2)}) collective-permute-start(f32[8,16,512]{2,0,1:T(8,128)S(1)} %get-tuple-element.15), channel_id=1, source_target_pairs={{0,30},{2,0},{4,2},{6,4},{8,6},{10,8},{12,10},{14,12},{16,14},{18,... | collective-permute-start | bytes 786440 | tf_op jit(solution)/shard_map/ppermute | solution.py:257
  99.5 46.7 %collective-permute-start.9 = (f32[8,16,512]{2,0,1:T(8,128)S(1)}, f32[8,16,512]{2,0,1:T(8,128)S(1)}, u32[]{:S(2)}, u32[]{:S(2)}) collective-permute-start(f32[8,16,512]{2,0,1:T(8,128)S(1)} %get-tuple-element.16), channel_id=1, source_target_pairs={{0,4},{2,6},{4,8},{6,10},{8,12},{10,14},{12,16},{14,18},{16,20},{1... | collective-permute-start | bytes 786440 | tf_op jit(solution)/shard_map/ppermute | solution.py:257
Sparse Core Ops, SparseCore 0:
  50.2 37.6 reduce-scatter.4

commit v2 on v1

v2 whole, which is shorter than its diff:
```python
import functools

import jax
import jax.numpy as jnp
from jax import lax
from jax.experimental import pallas as pl
from jax.experimental.pallas import tpu as pltpu
from jax.sharding import PartitionSpec as P

SHIFT = 32
view_offsets = (-2, -1, 1, 2)
MESH = pl.DeviceIdType.MESH
VMEM = pl.BlockSpec(memory_space=pltpu.VMEM)


def banded(kernel, height):
    taps = jnp.transpose(kernel, (4, 0, 2, 3, 1))
    zero = jnp.zeros((), kernel.dtype)
    rows = []
    for h in range(height):
        rows.append(lax.pad(taps, zero, [(0, 0, 0)] * 3 + [(h - 1, height - 2 - h, 0)] + [(0, 0, 0)]))
    return jnp.stack(rows, axis=1)


def flipped(kernel):
    return jnp.transpose(jnp.flip(kernel, (2, 3, 4)), (1, 0, 2, 3, 4))


def mul(a, b):
    return jnp.dot(a, b, preferred_element_type=jnp.float32)


def mul_t(a, b):
    return lax.dot_general(a, b, (((1,), (1,)), ((), ())), preferred_element_type=jnp.float32)


def lanes(width):
    return lax.broadcasted_iota(jnp.int32, (1, width), 1)


def from_left(x):
    width = x.shape[1]
    return jnp.where(lanes(width) > 0, pltpu.roll(x, 1, 1), 0.0)


def from_right(x):
    width = x.shape[1]
    return jnp.where(lanes(width) < width - 1, pltpu.roll(x, width - 1, 1), 0.0)


SMALL = 64


def turned(x, by):
    count, width = x.shape
    parts = []
    for start in range(0, width, 256):
        before = (start - 128) % width
        after = (start + 256) % width
        parts.append(
            jnp.concatenate(
                [x[:, before : before + 128], x[:, start : start + 256], x[:, after : after + 128]], axis=1
            )
        )
    source = lax.broadcasted_iota(jnp.int32, (512, 256), 0) - 128
    target = lax.broadcasted_iota(jnp.int32, (512, 256), 1)
    pick = jnp.where(source - target == by, 1.0, 0.0).astype(x.dtype)
    out = mul(jnp.concatenate(parts, axis=0), pick)
    return jnp.concatenate([out[i * count : (i + 1) * count] for i in range(width // 256)], axis=1)


def compute(
    dims,
    feat_ref, cot_ref, ints_ref, floats_ref, b1_ref, b2_ref, b3_ref, bias_ref,
    grad_ref, wsum_ref,
    bands, halo, ints_in, floats_in, ints, floats,
    warp, mean, cost, scot, spre, hid, acc1, acc2, cg, pad, taps,
    own_grad, out_grad, a_send, a_recv, b_send, b_recv, c_send, c_recv, ar, ar_in,
    send_sem, recv_sem, local_sem,
):
    chans, mid, height, held, width, own, planes, cams = dims
    top = (held - height) // 2
    lead = held - height - 1
    half = chans // 2
    band = height * chans
    mband = height * mid
    steps = ar_in.shape[0]

    cam = lax.axis_index("cam")
    me = lax.axis_index("depth")
    other = 1 - me
    first_own = (planes - own) * me
    odd = lax.rem(cam, 2)

    def at(offset):
        return lax.rem(cam + cams + offset * (2 * odd - 1), cams)

    def slot(t):
        return t + odd * (3 - 2 * t)

    mate = at(-1)
    partners = []
    reach = 1
    while reach < cams:
        bit = lax.rem(cam // reach, 2)
        partners.append((cam + reach * (1 - 2 * bit), me))
        reach *= 2
    partners.append((cam, other))

    barrier = pltpu.get_barrier_semaphore()
    greeted = [(at(-2), me), (at(-1), me), (at(1), me), (at(2), me)] + partners
    for device in greeted:
        pl.semaphore_signal(barrier, inc=1, device_id=device, device_id_type=MESH)
    pl.semaphore_wait(barrier, len(greeted))

    started = []

    def remote(n, src, dst, device):
        return pltpu.make_async_remote_copy(
            src_ref=src, dst_ref=dst, send_sem=send_sem.at[n], recv_sem=recv_sem.at[n],
            device_id=device, device_id_type=MESH,
        )

    def begin(copy):
        copy.start()
        started.append(copy)
        return copy

    edge = pl.multiple_of((own - 2) * other * mband, mband)
    ints_copy = begin(remote(0, ints_ref, ints_in, (cam, other)))
    floats_copy = begin(remote(1, floats_ref, floats_in, (cam, other)))
    feat1 = begin(remote(4, feat_ref, bands.at[1], (at(1), me)))
    feat2 = begin(remote(5, feat_ref, bands.at[2], (mate, me)))
    halo_copy = begin(remote(2, cot_ref.at[pl.ds(edge, 2 * mband), :], halo, (cam, other)))
    feat0 = begin(remote(3, feat_ref, bands.at[0], (at(-2), me)))
    own_ints = pltpu.make_async_copy(ints_ref, ints.at[me], local_sem.at[0])
    own_floats = pltpu.make_async_copy(floats_ref, floats.at[me], local_sem.at[1])
    own_ints.start()
    own_floats.start()

    for end in (0, planes + 1):
        scot[end * 3 * mband : (end + 1) * 3 * mband, :] = jnp.zeros((3 * mband, width), scot.dtype)
        spre[end * 3 * mband : (end + 1) * 3 * mband, :] = jnp.zeros((3 * mband, width), spre.dtype)
        cost[end * band : (end + 1) * band, :] = jnp.zeros((band, width), cost.dtype)

    def shift_plane(plane, p):
        wide = plane.astype(jnp.float32)
        base = pl.multiple_of((p + 1) * 3 * mband, mband)
        scot[pl.ds(base, mband), :] = from_left(wide).astype(scot.dtype)
        scot[pl.ds(base + mband, mband), :] = plane
        scot[pl.ds(base + 2 * mband, mband), :] = from_right(wide).astype(scot.dtype)

    for i in range(own):
        shift_plane(cot_ref[i * mband : (i + 1) * mband, :], first_own + i)

    own_ints.wait()
    own_floats.wait()
    ints_copy.wait_recv()
    floats_copy.wait_recv()
    more_ints = pltpu.make_async_copy(ints_in, ints.at[other], local_sem.at[2])
    more_floats = pltpu.make_async_copy(floats_in, floats.at[other], local_sem.at[3])
    more_ints.start()
    more_floats.start()
    halo_copy.wait_recv()
    for i in range(2):
        shift_plane(halo[i * mband : (i + 1) * mband, :], own * other + i)
    more_ints.wait()
    more_floats.wait()

    inv = floats[me, 4, SMALL]

    def place(p):
        at_plane = p + me * (2 * own - planes)
        return at_plane // own, lax.rem(at_plane, own)

    def row_of(s, p):
        slab, lane = place(p)
        return ints[slab, s, lane]

    def weights(s, p):
        slab, lane = place(p)
        c = ints[slab, s + 4, lane]
        fy = floats[slab, s, lane]
        fx = floats[slab, s + 4, lane]
        spot = lanes(width) + c
        left = jnp.where((spot >= 0) & (spot < width), 1.0 - fx, 0.0)
        right = jnp.where((spot >= -1) & (spot < width - 1), fx, 0.0)
        return c, fy, left, right

    def warp_slot(t, last):
        s = slot(t)

        def plane(p, _):
            c, fy, left, right = weights(s, p)
            r = row_of(s, p)
            window = bands[t, : band + chans, :]
            for k in range(1, lead + 1):
                window = jnp.where(r == k, bands[t, k * chans : band + (k + 1) * chans, :], window)
            here = turned(window, c)
            for h in range(height):
                rows = slice(h * chans, (h + 1) * chans)
                mixed = (1.0 - fy) * here[rows] + fy * here[(h + 1) * chans : (h + 2) * chans]
                warped = left * mixed + right * pltpu.roll(mixed, width - 1, 1)
                warp[t, p, rows, :] = warped
                if last:
                    ref = feat_ref[(top + h) * chans : (top + h + 1) * chans, :].astype(jnp.float32)
                    first = ref
                    second = ref * ref
                    for u in range(4):
                        view = warped if u == t else warp[u, p, rows, :]
                        weighted = floats[me, slot(u), SMALL] * view
                        first = first + weighted
                        second = second + weighted * view
                    average = first * inv
                    mean[p, rows, :] = average
                    spot = pl.multiple_of((p + 1) * band + h * chans, chans)
                    cost[pl.ds(spot, chans), :] = (second * inv - average * average).astype(cost.dtype)
            return 0

        lax.fori_loop(0, planes, plane, 0)

    feat2.wait_recv()
    warp_slot(2, False)
    feat1.wait_recv()
    feat3 = begin(remote(6, bands.at[1], bands.at[3], (mate, me)))
    warp_slot(1, False)
    feat3.wait_recv()
    warp_slot(3, False)
    feat0.wait_recv()
    warp_slot(0, True)

    def middle(i, _):
        p = first_own // 2 + i
        x = cost[pl.ds(pl.multiple_of(p * band, band), 3 * band), :]
        parts = mul(b1_ref[...], x)
        pre = from_left(parts[:mband]) + parts[mband : 2 * mband] + from_right(parts[2 * mband :])
        pre = pre + bias_ref[...]
        gate = jax.nn.sigmoid(pre)
        hid[pl.ds(pl.multiple_of(p * mband, mband), mband), :] = (pre * gate).astype(hid.dtype)
        y = scot[pl.ds(pl.multiple_of(p * 3 * mband, 3 * mband), 3 * 3 * mband), :]
        back = mul(b2_ref[...], y) * (gate * (1.0 + pre * (1.0 - gate)))
        base = pl.multiple_of((p + 1) * 3 * mband, mband)
        spre[pl.ds(base, mband), :] = from_left(back).astype(spre.dtype)
        spre[pl.ds(base + mband, mband), :] = back.astype(spre.dtype)
        spre[pl.ds(base + 2 * mband, mband), :] = from_right(back).astype(spre.dtype)
        return 0

    lax.fori_loop(0, own + (planes - own) // 2, middle, 0)

    acc1[...] = jnp.zeros_like(acc1)
    acc2[...] = jnp.zeros_like(acc2)
    own_grad[...] = jnp.zeros_like(own_grad)

    def back_plane(i, _):
        p = first_own + i
        s3 = spre[pl.ds(pl.multiple_of(p * 3 * mband, 3 * mband), 9 * mband), :]
        c3 = scot[pl.ds(pl.multiple_of(p * 3 * mband, 3 * mband), 9 * mband), :]
        cg[i] = mul(b3_ref[...], s3) * (2.0 * inv)
        acc1[...] += mul_t(s3, cost[pl.ds(pl.multiple_of((p + 1) * band, band), band), :])
        acc2[:, :mband] += mul_t(c3, hid[pl.ds(pl.multiple_of(p * mband, mband), mband), :])
        return 0

    lax.fori_loop(0, own, back_plane, 0)

    def fold(acc, block, offset):
        rows = acc[...].reshape(9, height, mid, 128)
        lane = lax.broadcasted_iota(jnp.int32, (1, 1, 128), 2)
        total = None
        for g in range(height):
            ok = (lane >= (g - 1) * block) & (lane < (g + 2) * block) & (lane < height * block)
            part = jnp.where(ok, rows[:, g], 0.0).reshape(9 * mid, 128)
            turn = (offset - (g - 1) * block) % 128
            if turn:
                part = pltpu.roll(part, turn, 1)
            total = part if total is None else total + part
        return total

    ar[0] = fold(acc1, chans, 0) + fold(acc2, mid, 3 * chans)
    reduce_copies = []

    def reduce_begin():
        k = len(reduce_copies)
        if k < steps:
            reduce_copies.append(begin(remote(14 + k, ar.at[k], ar_in.at[k], partners[k])))

    def reduce_next():
        k = len(reduce_copies)
        if k <= steps and k > 0:
            reduce_copies[k - 1].wait_recv()
            ar[k] = ar[k - 1] + ar_in[k - 1]

    reduce_begin()

    def slot_back(t, emit):
        s = slot(t)
        weight = floats[me, s, SMALL]

        def plane(i, _):
            p = first_own + i
            c, fy, left, right = weights(s, p)
            carried = None
            for h in range(height):
                rows = slice(h * chans, (h + 1) * chans)
                grad = (weight * cg[i, rows, :]) * (warp[t, p, rows, :] - mean[p, rows, :])
                taps[rows, :] = (left * grad + pltpu.roll(right * grad, 1, 1)).astype(taps.dtype)
            spread = turned(taps[...], -c)
            for h in range(height):
                rows = slice(h * chans, (h + 1) * chans)
                value = (1.0 - fy) * spread[rows]
                if carried is not None:
                    value = value + carried
                carried = fy * spread[rows]
                pad[i, rows, :] = value
            pad[i, height * chans :, :] = carried
            return 0

        lax.fori_loop(0, own, plane, 0)
        starts = [row_of(s, first_own + i) for i in range(own)]
        for r in range(held):
            total = None
            for i in range(own):
                part = jnp.zeros((chans, width), pad.dtype)
                for k in range(lead + 1):
                    if 0 <= r - k <= height:
                        row = pad[i, (r - k) * chans : (r - k + 1) * chans, :]
                        part = jnp.where(starts[i] == k, row, part)
                total = part if total is None else total + part
            for e in range(2):
                emit(e, slice(r * half, (r + 1) * half), total[e * half : (e + 1) * half])

    def to_mate(n):
        def emit(e, rows, value):
            a_send[n, e, rows, :] = value.astype(a_send.dtype)

        return emit

    def outward(n):
        def emit(e, rows, value):
            out_grad[n, e, rows, :] = value

        return emit

    slot_back(3, to_mate(1))
    a1 = begin(remote(8, a_send.at[1], a_recv.at[1], (mate, me)))
    reduce_next()
    reduce_begin()
    slot_back(2, to_mate(0))
    a0 = begin(remote(7, a_send.at[0], a_recv.at[0], (mate, me)))
    reduce_next()
    reduce_begin()
    slot_back(0, outward(0))
    b_send[0] = out_grad[0, other].astype(b_send.dtype)
    b0 = begin(remote(9, b_send.at[0], b_recv.at[0], (cam, other)))
    reduce_next()
    reduce_begin()
    slot_back(1, outward(1))
    a1.wait_recv()
    b_send[1] = (out_grad[1, other] + a_recv[1, other].astype(jnp.float32)).astype(b_send.dtype)
    b1 = begin(remote(10, b_send.at[1], b_recv.at[1], (cam, other)))
    reduce_next()
    reduce_begin()

    for h in range(height):
        rows = slice(h * chans, (h + 1) * chans)
        ref = feat_ref[(top + h) * chans : (top + h + 1) * chans, :].astype(jnp.float32)
        total = None
        for i in range(own):
            part = cg[i, rows, :] * (ref - mean[first_own + i, rows, :])
            total = part if total is None else total + part
        for e in range(2):
            own_grad[e, (top + h) * half : (top + h + 1) * half, :] = total[e * half : (e + 1) * half]
    a0.wait_recv()
    b_send[2] = (own_grad[other] + a_recv[0, other].astype(jnp.float32)).astype(b_send.dtype)
    b2 = begin(remote(11, b_send.at[2], b_recv.at[2], (cam, other)))

    b0.wait_recv()
    c_send[0] = (out_grad[0, me] + b_recv[0].astype(jnp.float32)).astype(c_send.dtype)
    c0 = begin(remote(12, c_send.at[0], c_recv.at[0], (at(2), me)))
    b1.wait_recv()
    c_send[1] = (
        out_grad[1, me] + a_recv[1, me].astype(jnp.float32) + b_recv[1].astype(jnp.float32)
    ).astype(c_send.dtype)
    c1 = begin(remote(13, c_send.at[1], c_recv.at[1], (at(1), me)))
    while len(reduce_copies) < steps:
        reduce_next()
        reduce_begin()
    reduce_next()
    wsum_ref[...] = ar[steps]
    b2.wait_recv()
    own_grad[me] = own_grad[me] + a_recv[0, me].astype(jnp.float32) + b_recv[2].astype(jnp.float32)
    c0.wait_recv()
    c1.wait_recv()
    grad_ref[...] = own_grad[me] + (c_recv[0].astype(jnp.float32) + c_recv[1].astype(jnp.float32))
    for copy in started:
        copy.wait_send()


def shards(
    features, view_mask, row_offset, frac_row, col_offset, frac_col,
    first_kernel, first_bias, second_kernel, cotangent,
):
    cams, slabs = lax.axis_size("cam"), lax.axis_size("depth")
    _, chans, held, width = features.shape
    mid = first_kernel.shape[0]
    _, _, own, height, _ = cotangent.shape
    band, mband, half = height * chans, height * mid, chans // 2
    assert slabs == 2 and 2 <= own <= 64 and band == 128 and width % 256 == 0 and cams & (cams - 1) == 0
    planes = own + 2
    steps = cams.bit_length()

    feat = jnp.transpose(features[0], (1, 0, 2)).reshape(held * chans, width)
    cot = jnp.transpose(cotangent[0], (1, 2, 0, 3)).reshape(own * mband, width)
    mask = view_mask[0].astype(jnp.float32)
    inv = 1.0 / (1.0 + jnp.sum(mask))
    wide = ((0, 0), (0, SMALL - own))
    ints = jnp.pad(jnp.concatenate([row_offset[0], col_offset[0]]), ((0, 0), (0, 128 - own)))
    small = jnp.concatenate([mask, jnp.broadcast_to(inv, (4,))])[:, None]
    floats = jnp.concatenate(
        [
            jnp.pad(jnp.concatenate([frac_row[0], frac_col[0]]), wide),
            jnp.pad(small, ((0, 0), (0, 127 - SMALL))),
        ],
        axis=1,
    )

    b1 = banded(first_kernel, height).reshape(3 * mband, 3 * band)
    b2 = jnp.transpose(banded(flipped(second_kernel), height), (1, 2, 3, 0, 4, 5)).reshape(mband, 9 * mband)
    b3 = jnp.transpose(banded(flipped(first_kernel), height), (1, 2, 3, 0, 4, 5)).reshape(band, 9 * mband)
    bias = jnp.tile(first_bias, height).reshape(mband, 1)

    f32, bf16, i32 = jnp.float32, jnp.bfloat16, jnp.int32
    rows = held * half
    grads, wsum = pl.pallas_call(
        functools.partial(compute, (chans, mid, height, held, width, own, planes, cams)),
        out_shape=(
            jax.ShapeDtypeStruct((rows, width), f32),
            jax.ShapeDtypeStruct((9 * mid, 128), f32),
        ),
        in_specs=[VMEM] * 8,
        out_specs=(VMEM, VMEM),
        scratch_shapes=[
            pltpu.VMEM((4, held * chans, width), bf16),
            pltpu.VMEM((2 * mband, width), bf16),
            pltpu.VMEM((8, 128), i32),
            pltpu.VMEM((8, 128), f32),
            pltpu.SMEM((2, 8, 128), i32),
            pltpu.SMEM((2, 8, 128), f32),
            pltpu.VMEM((4, planes, band, width), f32),
            pltpu.VMEM((planes, band, width), f32),
            pltpu.VMEM(((planes + 2) * band, width), bf16),
            pltpu.VMEM(((planes + 2) * 3 * mband, width), bf16),
            pltpu.VMEM(((planes + 2) * 3 * mband, width), bf16),
            pltpu.VMEM((planes * mband, width), bf16),
            pltpu.VMEM((9 * mband, 128), f32),
            pltpu.VMEM((9 * mband, 128), f32),
            pltpu.VMEM((own, band, width), f32),
            pltpu.VMEM((own, band + chans, width), f32),
            pltpu.VMEM((band, width), bf16),
            pltpu.VMEM((2, rows, width), f32),
            pltpu.VMEM((2, 2, rows, width), f32),
            pltpu.VMEM((2, 2, rows, width), bf16),
            pltpu.VMEM((2, 2, rows, width), bf16),
            pltpu.VMEM((3, rows, width), bf16),
            pltpu.VMEM((3, rows, width), bf16),
            pltpu.VMEM((2, rows, width), bf16),
            pltpu.VMEM((2, rows, width), bf16),
            pltpu.VMEM((steps + 1, 9 * mid, 128), f32),
            pltpu.VMEM((steps, 9 * mid, 128), f32),
            pltpu.SemaphoreType.DMA((14 + steps,)),
            pltpu.SemaphoreType.DMA((14 + steps,)),
            pltpu.SemaphoreType.DMA((4,)),
        ],
        compiler_params=pltpu.CompilerParams(
            vmem_limit_bytes=48 * 2**20, collective_id=0, has_side_effects=True
        ),
        name="core",
    )(feat, cot, ints, floats, b1, b2, b3, bias)

    feature_grad = jnp.transpose(grads.reshape(held, half, width), (1, 0, 2))
    scale = (cams * slabs * own * height * width) ** (-0.5)
    taps = (wsum * scale).reshape(3, 3, mid, 128)[::-1, ::-1]
    first = taps[..., : 3 * chans].reshape(3, 3, mid, 3, chans)
    second = taps[..., 3 * chans : 3 * chans + 3 * mid].reshape(3, 3, mid, 3, mid)
    order = (2, 4, 0, 3, 1)
    return feature_grad[None], jnp.transpose(first, order), jnp.transpose(second, order)


def solution(mesh):
    placed = (
        P("cam", None, None, None),
        P("cam", None),
        P("cam", None, "depth"),
        P("cam", None, "depth"),
        P("cam", None, "depth"),
        P("cam", None, "depth"),
        P(),
        P(),
        P(),
        P("cam", None, "depth", None, None),
    )
    return jax.shard_map(
        shards,
        mesh=mesh,
        in_specs=placed,
        out_specs=(P("cam", "depth", None, None), P(), P()),
        check_vma=False,
    )
```

time: 154 us -> 60.1 us (0.39)
  blocking collectives: 45 us -> 0 us
  waiting for transfers between devices: 41.6 us -> 0 us
  Pallas kernels: 16.9 us -> 46.1 us
  starting transfers between devices: 18.1 us -> 0 us
  between operations: 15 us -> 1.51 us
  other arithmetic: 5.26 us -> 0.96 us
  local copies, waits for them, and re-layouts: 12 us -> 10.4 us
    psum x1 -> x0, blocking collectives: 45 us -> none  [shards(): wsum = lax.psum(wsum, ('cam', 'depth'))]
    unnamed x2 -> x0, waiting for transfers between devices: 37.9 us -> none
    pallas_call x1, Pallas kernels: 16.9 us -> 46.1 us  [shards(): pl.pallas_call(functools.partial(compute, (chans, mid, height, held, widt...]
    ppermute x10 -> x0, starting transfers between devices: 18 us -> none  [the longest x4 8.69 us: shards(): lax.ppermute(part[s + 1], 'cam', [(i, (i + offset) % cams) for i in range...]
    ppermute x10 -> x0, waiting for transfers between devices: 3.69 us -> none  [the longest x2 3.67 us: widened(): other = lax.ppermute(edge, 'depth', swap)]
    unnamed x15 -> x22, local copies, waits for them, and re-layouts: 6.21 us -> 6.76 us
  transfers between devices with their start and end apart: 11 -> 0, of which waited for: 2 -> 0; matrix products, arithmetic and copies ran while one was open for 7% -> 0% of each run, Pallas kernels for 0% -> 0%
where the time goes in v2:
time: 60.1 us; the launch traced here: 58.9 us
  Pallas kernels  46.1 us (77%)
  local copies, waits for them, and re-layouts  10.4 us (17%)
  between operations  1.51 us (3%)
  other arithmetic  0.96 us (2%)
    pallas_call x1, Pallas kernels, shards(): pl.pallas_call(functools.partial(compute, (chans, mid, height, held, widt...  46.1 us
    unnamed x22, local copies, waits for them, and re-layouts  6.76 us

profile of v2, /device:TPU:0, one launch (start us, length us, event | category | flops | bytes accessed | tf_op | source)
XLA Modules:
  0.0 58.9 jit_solution(16009295143470973894)
XLA Ops:
  0.6 0.8 %reverse_bitcast_fusion = bf16[3,32,3,3,8]{1,4,0,3,2:T(8,128)(2,1)S(1)} fusion(bf16[8,32,3,3,3]{1,0,4,3,2:T(8,128)(2,1)} %param.16), kind=kLoop, calls=%fused_computation.22 | loop fusion | bytes 27648 | tf_op jit(solution)/shard_map/transpose;transpose | solution.py:17
  1.5 0.1 maximum_bitcast_fusion.1
  1.6 0.2 copy.26
  1.8 0.2 reshape.39
  2.0 0.1 copy.27.b3_ref
  2.1 0.7 %copy-done.3 = bf16[8,8,3,3,3]{1,0,4,3,2:T(8,128)(2,1)S(1)} copy-done((bf16[8,8,3,3,3]{1,0,4,3,2:T(8,128)(2,1)S(1)}, bf16[8,8,3,3,3]{1,0,4,3,2:T(8,128)(2,1)}, u32[]{:S(2)}) %copy-start.3) | copy-done | bytes 3480
  2.8 0.1 maximum_bitcast_fusion
  2.9 0.2 copy.25
  3.1 0.2 reshape.38.b2_ref
  3.3 0.6 %copy-done.1 = bf16[8,32,3,3,3]{1,0,4,3,2:T(8,128)(2,1)S(1)} copy-done((bf16[8,32,3,3,3]{1,0,4,3,2:T(8,128)(2,1)S(1)}, bf16[8,32,3,3,3]{1,0,4,3,2:T(8,128)(2,1)}, u32[]{:S(2)}) %copy-start.1) | copy-done | bytes 13848
  4.0 0.1 pad_maximum_fusion
  4.1 0.1 copy.24
  4.2 0.2 reshape.37.b1_ref
  4.4 0.7 %copy-done = bf16[1,32,8,512]{3,2,1,0:T(8,128)(2,1)S(1)} copy-done((bf16[1,32,8,512]{3,2,1,0:T(8,128)(2,1)S(1)}, bf16[1,32,8,512]{3,2,1,0:T(8,128)(2,1)}, u32[]{:S(2)}) %copy-start) | copy-done | bytes 262168
  5.2 0.1 copy.21
  5.2 0.8 %copy-done.2 = bf16[1,8,4,4,512]{4,3,2,1,0:T(4,128)(2,1)S(1)} copy-done((bf16[1,8,4,4,512]{4,3,2,1,0:T(4,128)(2,1)S(1)}, bf16[1,8,4,4,512]{4,3,2,1,0:T(4,128)(2,1)}, u32[]{:S(2)}) %copy-start.2) | copy-done | bytes 131096
  6.1 0.1 copy.22
  6.1 0.6 %copy-done.8 = f32[8]{0:T(128)S(1)} copy-done((f32[8]{0:T(128)S(1)}, f32[8]{0:T(128)}, u32[]{:S(2)}) %copy-start.8) | copy-done | bytes 56
  6.8 0.1 reshape_tile.4.bias_ref
  6.9 0.6 copy-done.9
  7.5 0.6 %convert_reduce_fusion = f32[]{:T(128)} fusion(s32[1,4]{1,0:T(1,128)S(1)} %copy-done.9), kind=kLoop, calls=%fused_computation.31 | loop fusion | flops 7 | bytes 20 | tf_op jit(solution)/shard_map/reduce_sum | solution.py:414
  8.8 0.1 copy.23
  8.9 0.6 copy-done.5
  9.5 0.1 copy-done.4
  9.6 0.6 %copy-done.7 = s32[1,4,4]{2,1,0:T(4,128)S(1)} copy-done((s32[1,4,4]{2,1,0:T(4,128)S(1)}, s32[1,4,4]{2,1,0:T(4,128)}, u32[]{:S(2)}) %copy-start.7) | copy-done | bytes 88
  10.2 0.1 copy-done.6
  10.3 46.1 %core.1 = (f32[128,512]{1,0:T(8,128)S(1)}, f32[72,128]{1,0:T(8,128)S(1)}) custom-call(bf16[256,512]{1,0:T(8,128)(2,1)S(1)} %bitcast.65, bf16[128,512]{1,0:T(8,128)(2,1)S(1)} %bitcast.66, s32[8,128]{1,0:T(8,128)S(1)} %pad.67.ints_ref, f32[8,128]{1,0:T(8,128)S(1)} %select_maximum_fusion.floats_ref, bf16[96,384]{1,0:T(8,128)(2,1)S(1)} %reshape.37.b1_ref, ...), custom_call_target="tpu_custom_call" | custom-call | tf_op jit(solution)/shard_map/core/pallas_call | solution.py:433
  56.5 0.1 reshape.43
  56.7 0.7 %copy.31 = f32[8,8,3,3,3]{1,0,4,3,2:T(8,128)} copy(f32[8,8,3,3,3]{1,3,0,4,2:T(4,128)S(1)} %bitcast.68) | data formatting | bytes 13824
  57.3 0.1 reshape.42
  57.4 0.7 %copy.30 = f32[8,32,3,3,3]{1,0,4,3,2:T(8,128)} copy(f32[8,32,3,3,3]{1,3,0,4,2:T(4,128)S(1)} %bitcast.69) | data formatting | bytes 55296
  58.1 0.9 %copy.33 = f32[8,16,512]{2,0,1:T(8,128)} copy(f32[8,16,512]{2,1,0:T(8,128)S(1)} %bitcast.67) | data formatting | bytes 524288 | tf_op jit(solution)/shard_map/reshape | solution.py:479
  (25 shorter events, 0.4 us)
Async XLA Ops:
  1.9 0.8 %copy-start.3 = (bf16[8,8,3,3,3]{1,0,4,3,2:T(8,128)(2,1)S(1)}, bf16[8,8,3,3,3]{1,0,4,3,2:T(8,128)(2,1)}, u32[]{:S(2)}) copy-start(bf16[8,8,3,3,3]{1,0,4,3,2:T(8,128)(2,1)} %param.18) | copy-start | bytes 10372
  3.1 0.8 %copy-start.1 = (bf16[8,32,3,3,3]{1,0,4,3,2:T(8,128)(2,1)S(1)}, bf16[8,32,3,3,3]{1,0,4,3,2:T(8,128)(2,1)}, u32[]{:S(2)}) copy-start(bf16[8,32,3,3,3]{1,0,4,3,2:T(8,128)(2,1)} %param.16) | copy-start | bytes 41476
  4.2 1.0 %copy-start = (bf16[1,32,8,512]{3,2,1,0:T(8,128)(2,1)S(1)}, bf16[1,32,8,512]{3,2,1,0:T(8,128)(2,1)}, u32[]{:S(2)}) copy-start(bf16[1,32,8,512]{3,2,1,0:T(8,128)(2,1)} %param.10) | copy-start | bytes 786436
  5.1 0.9 %copy-start.2 = (bf16[1,8,4,4,512]{4,3,2,1,0:T(4,128)(2,1)S(1)}, bf16[1,8,4,4,512]{4,3,2,1,0:T(4,128)(2,1)}, u32[]{:S(2)}) copy-start(bf16[1,8,4,4,512]{4,3,2,1,0:T(4,128)(2,1)} %param.19) | copy-start | bytes 393220
  6.1 0.7 %copy-start.8 = (f32[8]{0:T(128)S(1)}, f32[8]{0:T(128)}, u32[]{:S(2)}) copy-start(f32[8]{0:T(128)} %param.17) | copy-start | bytes 100
  6.8 0.7 %copy-start.9 = (s32[1,4]{1,0:T(1,128)S(1)}, s32[1,4]{1,0:T(1,128)}, u32[]{:S(2)}) copy-start(s32[1,4]{1,0:T(1,128)} %param.11) | copy-start | bytes 52
  8.8 0.7 %copy-start.5 = (f32[1,4,4]{2,1,0:T(4,128)S(1)}, f32[1,4,4]{2,1,0:T(4,128)}, u32[]{:S(2)}) copy-start(f32[1,4,4]{2,1,0:T(4,128)} %param.13) | copy-start | bytes 196
  8.9 0.7 %copy-start.4 = (f32[1,4,4]{2,1,0:T(4,128)S(1)}, f32[1,4,4]{2,1,0:T(4,128)}, u32[]{:S(2)}) copy-start(f32[1,4,4]{2,1,0:T(4,128)} %param.15) | copy-start | bytes 196
  9.6 0.7 %copy-start.7 = (s32[1,4,4]{2,1,0:T(4,128)S(1)}, s32[1,4,4]{2,1,0:T(4,128)}, u32[]{:S(2)}) copy-start(s32[1,4,4]{2,1,0:T(4,128)} %param.12) | copy-start | bytes 196
  9.6 0.7 %copy-start.6 = (s32[1,4,4]{2,1,0:T(4,128)S(1)}, s32[1,4,4]{2,1,0:T(4,128)}, u32[]{:S(2)}) copy-start(s32[1,4,4]{2,1,0:T(4,128)} %param.14) | copy-start | bytes 196

commit v3 on v2

--- a/solution.py
+++ b/solution.py
@@ -7,23 +7,10 @@
 from jax.experimental.pallas import tpu as pltpu
 from jax.sharding import PartitionSpec as P
 
-SHIFT = 32
 view_offsets = (-2, -1, 1, 2)
 MESH = pl.DeviceIdType.MESH
+SMEM = pl.BlockSpec(memory_space=pltpu.SMEM)
 VMEM = pl.BlockSpec(memory_space=pltpu.VMEM)
-
-
-def banded(kernel, height):
-    taps = jnp.transpose(kernel, (4, 0, 2, 3, 1))
-    zero = jnp.zeros((), kernel.dtype)
-    rows = []
-    for h in range(height):
-        rows.append(lax.pad(taps, zero, [(0, 0, 0)] * 3 + [(h - 1, height - 2 - h, 0)] + [(0, 0, 0)]))
-    return jnp.stack(rows, axis=1)
-
-
-def flipped(kernel):
-    return jnp.transpose(jnp.flip(kernel, (2, 3, 4)), (1, 0, 2, 3, 4))
 
 
 def mul(a, b):
@@ -46,9 +33,6 @@
 def from_right(x):
     width = x.shape[1]
     return jnp.where(lanes(width) < width - 1, pltpu.roll(x, width - 1, 1), 0.0)
-
-
-SMALL = 64
 
 
 def turned(x, by):
@@ -71,11 +55,12 @@
 
 def compute(
     dims,
-    feat_ref, cot_ref, ints_ref, floats_ref, b1_ref, b2_ref, b3_ref, bias_ref,
+    raw_ref, cotangent_ref, ints_ref, floats_ref, mask_ref, bias_ref, w1_ref, w2_ref,
     grad_ref, wsum_ref,
     bands, halo, ints_in, floats_in, ints, floats,
     warp, mean, cost, scot, spre, hid, acc1, acc2, cg, pad, taps,
     own_grad, out_grad, a_send, a_recv, b_send, b_recv, c_send, c_recv, ar, ar_in,
+    wide, cot_wide, feat_ref, cot_ref, b1_ref, b1_wide, b2_ref, b2_wide, b3_ref, b3_wide, bias,
     send_sem, recv_sem, local_sem,
 ):
     chans, mid, height, held, width, own, planes, cams = dims
@@ -111,6 +96,11 @@
     greeted = [(at(-2), me), (at(-1), me), (at(1), me), (at(2), me)] + partners
     for device in greeted:
         pl.semaphore_signal(barrier, inc=1, device_id=device, device_id_type=MESH)
+
+    wide[...] = raw_ref[...].astype(jnp.float32)
+    for r in range(held):
+        feat_ref[r * chans : (r + 1) * chans, :] = wide[:, r, :].astype(feat_ref.dtype)
+
     pl.semaphore_wait(barrier, len(greeted))
 
     started = []
@@ -126,17 +116,29 @@
         started.append(copy)
         return copy
 
-    edge = pl.multiple_of((own - 2) * other * mband, mband)
+    span = held // 2 * chans
+
+    def part(ref, e):
+        return ref.at[pl.ds(pl.multiple_of(e * span, span), span), :]
+
+    feat1 = begin(remote(4, part(feat_ref, me), part(bands.at[1], me), (at(1), me)))
+    feat0 = begin(remote(3, part(feat_ref, me), part(bands.at[0], me), (at(-2), me)))
+    feat2 = begin(remote(5, feat_ref, bands.at[2], (mate, me)))
     ints_copy = begin(remote(0, ints_ref, ints_in, (cam, other)))
     floats_copy = begin(remote(1, floats_ref, floats_in, (cam, other)))
-    feat1 = begin(remote(4, feat_ref, bands.at[1], (at(1), me)))
-    feat2 = begin(remote(5, feat_ref, bands.at[2], (mate, me)))
-    halo_copy = begin(remote(2, cot_ref.at[pl.ds(edge, 2 * mband), :], halo, (cam, other)))
-    feat0 = begin(remote(3, feat_ref, bands.at[0], (at(-2), me)))
     own_ints = pltpu.make_async_copy(ints_ref, ints.at[me], local_sem.at[0])
     own_floats = pltpu.make_async_copy(floats_ref, floats.at[me], local_sem.at[1])
     own_ints.start()
     own_floats.start()
+
+    for i in range(own):
+        cot_wide[:, i * height : (i + 1) * height, :] = cotangent_ref[:, i].astype(jnp.float32)
+    for i in range(own):
+        cot_ref[i * mband : (i + 1) * mband, :] = jnp.concatenate(
+            [cot_wide[:, i * height + h, :] for h in range(height)], axis=0
+        ).astype(cot_ref.dtype)
+    edge = pl.multiple_of((own - 2) * other * mband, mband)
+    halo_copy = begin(remote(2, cot_ref.at[pl.ds(edge, 2 * mband), :], halo, (cam, other)))
 
     for end in (0, planes + 1):
         scot[end * 3 * mband : (end + 1) * 3 * mband, :] = jnp.zeros((3 * mband, width), scot.dtype)
@@ -152,6 +154,49 @@
 
     for i in range(own):
         shift_plane(cot_ref[i * mband : (i + 1) * mband, :], first_own + i)
+
+    def blocks(w_ref, block, kd, kw):
+        taps = []
+        for kh in range(3):
+            tap = w_ref[kd, kh, kw].astype(jnp.float32)
+            taps.append(jnp.concatenate([tap, jnp.zeros((mid, 128 - block), jnp.float32)], axis=1))
+        found = []
+        for h in range(height):
+            total = None
+            for kh in range(3):
+                to = h + kh - 1
+                if 0 <= to < height:
+                    moved = taps[kh] if to == 0 else pltpu.roll(taps[kh], to * block, 1)
+                    total = moved if total is None else total + moved
+            found.append(total)
+        return found
+
+    for kd in range(3):
+        for kw in range(3):
+            for h, value in enumerate(blocks(w1_ref, chans, kd, kw)):
+                row = (kw * height + h) * mid
+                b1_wide[row : row + mid, kd * 128 : (kd + 1) * 128] = value
+                row = (((2 - kd) * 3 + 2 - kw) * height + h) * mid
+                b3_wide[row : row + mid, :] = value
+            for h, value in enumerate(blocks(w2_ref, mid, kd, kw)):
+                row = (((2 - kd) * 3 + 2 - kw) * height + h) * mid
+                b2_wide[row : row + mid, :] = value
+    for ref in (b2_wide, b3_wide):
+        ref[9 * mband :, :] = jnp.zeros((ref.shape[0] - 9 * mband, 128), jnp.float32)
+    b1_ref[...] = b1_wide[...].astype(b1_ref.dtype)
+    b2_ref[...] = jnp.transpose(b2_wide[...])[:mband].astype(b2_ref.dtype)
+    b3_ref[...] = jnp.transpose(b3_wide[...]).astype(b3_ref.dtype)
+    which = lax.rem(lax.broadcasted_iota(jnp.int32, (mband, width), 0), mid)
+    column = jnp.zeros((mband, width), jnp.float32)
+    for o in range(mid):
+        column = jnp.where(which == o, bias_ref[o], column)
+    bias[...] = column
+
+    def weight_of(s):
+        return mask_ref[s].astype(jnp.float32)
+
+    count = 1.0 + weight_of(0) + weight_of(1) + weight_of(2) + weight_of(3)
+    inv = 1.0 / jnp.full((1, width), count, jnp.float32)
 
     own_ints.wait()
     own_floats.wait()
@@ -166,8 +211,6 @@
         shift_plane(halo[i * mband : (i + 1) * mband, :], own * other + i)
     more_ints.wait()
     more_floats.wait()
-
-    inv = floats[me, 4, SMALL]
 
     def place(p):
         at_plane = p + me * (2 * own - planes)
@@ -208,7 +251,7 @@
                     second = ref * ref
                     for u in range(4):
                         view = warped if u == t else warp[u, p, rows, :]
-                        weighted = floats[me, slot(u), SMALL] * view
+                        weighted = weight_of(slot(u)) * view
                         first = first + weighted
                         second = second + weighted * view
                     average = first * inv
@@ -222,11 +265,17 @@
     feat2.wait_recv()
     warp_slot(2, False)
     feat1.wait_recv()
-    feat3 = begin(remote(6, bands.at[1], bands.at[3], (mate, me)))
+    over1 = begin(remote(14, part(bands.at[1], me), part(bands.at[1], me), (cam, other)))
+    feat3 = begin(remote(6, part(bands.at[1], me), part(bands.at[3], me), (mate, me)))
+    feat0.wait_recv()
+    over0 = begin(remote(15, part(bands.at[0], me), part(bands.at[0], me), (cam, other)))
+    over1.wait_recv()
+    over3 = begin(remote(16, part(bands.at[1], other), part(bands.at[3], other), (mate, me)))
     warp_slot(1, False)
     feat3.wait_recv()
+    over3.wait_recv()
     warp_slot(3, False)
-    feat0.wait_recv()
+    over0.wait_recv()
     warp_slot(0, True)
 
     def middle(i, _):
@@ -234,11 +283,11 @@
         x = cost[pl.ds(pl.multiple_of(p * band, band), 3 * band), :]
         parts = mul(b1_ref[...], x)
         pre = from_left(parts[:mband]) + parts[mband : 2 * mband] + from_right(parts[2 * mband :])
-        pre = pre + bias_ref[...]
+        pre = pre + bias[...]
         gate = jax.nn.sigmoid(pre)
         hid[pl.ds(pl.multiple_of(p * mband, mband), mband), :] = (pre * gate).astype(hid.dtype)
         y = scot[pl.ds(pl.multiple_of(p * 3 * mband, 3 * mband), 3 * 3 * mband), :]
-        back = mul(b2_ref[...], y) * (gate * (1.0 + pre * (1.0 - gate)))
+        back = mul(b2_ref[:, : 9 * mband], y) * (gate * (1.0 + pre * (1.0 - gate)))
         base = pl.multiple_of((p + 1) * 3 * mband, mband)
         spre[pl.ds(base, mband), :] = from_left(back).astype(spre.dtype)
         spre[pl.ds(base + mband, mband), :] = back.astype(spre.dtype)
@@ -255,7 +304,7 @@
         p = first_own + i
         s3 = spre[pl.ds(pl.multiple_of(p * 3 * mband, 3 * mband), 9 * mband), :]
         c3 = scot[pl.ds(pl.multiple_of(p * 3 * mband, 3 * mband), 9 * mband), :]
-        cg[i] = mul(b3_ref[...], s3) * (2.0 * inv)
+        cg[i] = mul(b3_ref[:, : 9 * mband], s3) * (2.0 * inv)
         acc1[...] += mul_t(s3, cost[pl.ds(pl.multiple_of((p + 1) * band, band), band), :])
         acc2[:, :mband] += mul_t(c3, hid[pl.ds(pl.multiple_of(p * mband, mband), mband), :])
         return 0
@@ -281,7 +330,7 @@
     def reduce_begin():
         k = len(reduce_copies)
         if k < steps:
-            reduce_copies.append(begin(remote(14 + k, ar.at[k], ar_in.at[k], partners[k])))
+            reduce_copies.append(begin(remote(17 + k, ar.at[k], ar_in.at[k], partners[k])))
 
     def reduce_next():
         k = len(reduce_copies)
@@ -293,7 +342,7 @@
 
     def slot_back(t, emit):
         s = slot(t)
-        weight = floats[me, s, SMALL]
+        weight = weight_of(s)
 
         def plane(i, _):
             p = first_own + i
@@ -344,10 +393,6 @@
     a1 = begin(remote(8, a_send.at[1], a_recv.at[1], (mate, me)))
     reduce_next()
     reduce_begin()
-    slot_back(2, to_mate(0))
-    a0 = begin(remote(7, a_send.at[0], a_recv.at[0], (mate, me)))
-    reduce_next()
-    reduce_begin()
     slot_back(0, outward(0))
     b_send[0] = out_grad[0, other].astype(b_send.dtype)
     b0 = begin(remote(9, b_send.at[0], b_recv.at[0], (cam, other)))
@@ -357,6 +402,18 @@
     a1.wait_recv()
     b_send[1] = (out_grad[1, other] + a_recv[1, other].astype(jnp.float32)).astype(b_send.dtype)
     b1 = begin(remote(10, b_send.at[1], b_recv.at[1], (cam, other)))
+    b0.wait_recv()
+    c_send[0] = (out_grad[0, me] + b_recv[0].astype(jnp.float32)).astype(c_send.dtype)
+    c0 = begin(remote(12, c_send.at[0], c_recv.at[0], (at(2), me)))
+    reduce_next()
+    reduce_begin()
+    slot_back(2, to_mate(0))
+    a0 = begin(remote(7, a_send.at[0], a_recv.at[0], (mate, me)))
+    b1.wait_recv()
+    c_send[1] = (
+        out_grad[1, me] + a_recv[1, me].astype(jnp.float32) + b_recv[1].astype(jnp.float32)
+    ).astype(c_send.dtype)
+    c1 = begin(remote(13, c_send.at[1], c_recv.at[1], (at(1), me)))
     reduce_next()
     reduce_begin()
 
@@ -365,22 +422,13 @@
         ref = feat_ref[(top + h) * chans : (top + h + 1) * chans, :].astype(jnp.float32)
         total = None
         for i in range(own):
-            part = cg[i, rows, :] * (ref - mean[first_own + i, rows, :])
-            total = part if total is None else total + part
+            term = cg[i, rows, :] * (ref - mean[first_own + i, rows, :])
+            total = term if total is None else total + term
         for e in range(2):
             own_grad[e, (top + h) * half : (top + h + 1) * half, :] = total[e * half : (e + 1) * half]
     a0.wait_recv()
     b_send[2] = (own_grad[other] + a_recv[0, other].astype(jnp.float32)).astype(b_send.dtype)
     b2 = begin(remote(11, b_send.at[2], b_recv.at[2], (cam, other)))
-
-    b0.wait_recv()
-    c_send[0] = (out_grad[0, me] + b_recv[0].astype(jnp.float32)).astype(c_send.dtype)
-    c0 = begin(remote(12, c_send.at[0], c_recv.at[0], (at(2), me)))
-    b1.wait_recv()
-    c_send[1] = (
-        out_grad[1, me] + a_recv[1, me].astype(jnp.float32) + b_recv[1].astype(jnp.float32)
-    ).astype(c_send.dtype)
-    c1 = begin(remote(13, c_send.at[1], c_recv.at[1], (at(1), me)))
     while len(reduce_copies) < steps:
         reduce_next()
         reduce_begin()
@@ -408,35 +456,23 @@
     planes = own + 2
     steps = cams.bit_length()
 
-    feat = jnp.transpose(features[0], (1, 0, 2)).reshape(held * chans, width)
-    cot = jnp.transpose(cotangent[0], (1, 2, 0, 3)).reshape(own * mband, width)
-    mask = view_mask[0].astype(jnp.float32)
-    inv = 1.0 / (1.0 + jnp.sum(mask))
-    wide = ((0, 0), (0, SMALL - own))
-    ints = jnp.pad(jnp.concatenate([row_offset[0], col_offset[0]]), ((0, 0), (0, 128 - own)))
-    small = jnp.concatenate([mask, jnp.broadcast_to(inv, (4,))])[:, None]
-    floats = jnp.concatenate(
-        [
-            jnp.pad(jnp.concatenate([frac_row[0], frac_col[0]]), wide),
-            jnp.pad(small, ((0, 0), (0, 127 - SMALL))),
-        ],
-        axis=1,
-    )
-
-    b1 = banded(first_kernel, height).reshape(3 * mband, 3 * band)
-    b2 = jnp.transpose(banded(flipped(second_kernel), height), (1, 2, 3, 0, 4, 5)).reshape(mband, 9 * mband)
-    b3 = jnp.transpose(banded(flipped(first_kernel), height), (1, 2, 3, 0, 4, 5)).reshape(band, 9 * mband)
-    bias = jnp.tile(first_bias, height).reshape(mband, 1)
+    wide = ((0, 0), (0, 128 - own))
+    ints = jnp.pad(jnp.concatenate([row_offset[0], col_offset[0]]), wide)
+    floats = jnp.pad(jnp.concatenate([frac_row[0], frac_col[0]]), wide)
+    order = (2, 3, 4, 0, 1)
+    w1 = jnp.transpose(first_kernel, order)
+    w2 = jnp.transpose(second_kernel, order)
 
     f32, bf16, i32 = jnp.float32, jnp.bfloat16, jnp.int32
     rows = held * half
+    taps_rows = -(-9 * mband // 128) * 128
     grads, wsum = pl.pallas_call(
         functools.partial(compute, (chans, mid, height, held, width, own, planes, cams)),
         out_shape=(
             jax.ShapeDtypeStruct((rows, width), f32),
             jax.ShapeDtypeStruct((9 * mid, 128), f32),
         ),
-        in_specs=[VMEM] * 8,
+        in_specs=[VMEM] * 4 + [SMEM] * 2 + [VMEM] * 2,
         out_specs=(VMEM, VMEM),
         scratch_shapes=[
             pltpu.VMEM((4, held * chans, width), bf16),
@@ -466,15 +502,26 @@
             pltpu.VMEM((2, rows, width), bf16),
             pltpu.VMEM((steps + 1, 9 * mid, 128), f32),
             pltpu.VMEM((steps, 9 * mid, 128), f32),
-            pltpu.SemaphoreType.DMA((14 + steps,)),
-            pltpu.SemaphoreType.DMA((14 + steps,)),
+            pltpu.VMEM((chans, held, width), f32),
+            pltpu.VMEM((mid, own * height, width), f32),
+            pltpu.VMEM((held * chans, width), bf16),
+            pltpu.VMEM((own * mband, width), bf16),
+            pltpu.VMEM((3 * mband, 3 * band), bf16),
+            pltpu.VMEM((3 * mband, 3 * band), f32),
+            pltpu.VMEM((mband, taps_rows), bf16),
+            pltpu.VMEM((taps_rows, 128), f32),
+            pltpu.VMEM((band, taps_rows), bf16),
+            pltpu.VMEM((taps_rows, 128), f32),
+            pltpu.VMEM((mband, width), f32),
+            pltpu.SemaphoreType.DMA((17 + steps,)),
+            pltpu.SemaphoreType.DMA((17 + steps,)),
             pltpu.SemaphoreType.DMA((4,)),
         ],
         compiler_params=pltpu.CompilerParams(
             vmem_limit_bytes=48 * 2**20, collective_id=0, has_side_effects=True
         ),
         name="core",
-    )(feat, cot, ints, floats, b1, b2, b3, bias)
+    )(features[0], cotangent[0], ints, floats, view_mask[0], first_bias, w1, w2)
 
     feature_grad = jnp.transpose(grads.reshape(held, half, width), (1, 0, 2))
     scale = (cams * slabs * own * height * width) ** (-0.5)

time: 60.1 us -> 54.6 us (0.908); the launches traced: 58.9 us -> 54.3 us
  local copies, waits for them, and re-layouts: 10.4 us -> 7.98 us
  other arithmetic: 0.96 us -> 0.02 us
  between operations: 1.51 us -> 0.7 us
    another operation x8 -> x0, local copies, waits for them, and re-layouts: 1.15 us -> none  [the longest x2 0.84 us: banded(): taps = jnp.transpose(kernel, (4, 0, 2, 3, 1))]
    reshape x4 -> x0, local copies, waits for them, and re-layouts: 0.7 us -> none  [the longest x2 0.3 us: shards(): jnp.transpose(banded(flipped(first_kernel), height), (1, 2, 3, 0, 4, 5))]
where the time goes in v3:
time: 54.6 us; the launch traced here: 54.3 us
  Pallas kernels  45.6 us (84%)
  local copies, waits for them, and re-layouts  7.98 us (15%)
  between operations  0.7 us (1%)
    pallas_call x1, Pallas kernels, shards(): pl.pallas_call(functools.partial(compute, (chans, mid, height, held, widt...  45.6 us
    unnamed x22, local copies, waits for them, and re-layouts  6.8 us

profile of v3, /device:TPU:0, one launch (start us, length us, event | category | flops | bytes accessed | tf_op | source)
XLA Modules:
  0.0 54.3 jit_solution(17863674543314718286)
XLA Ops:
  0.6 0.0 copy-start.7
  0.6 0.0 copy-start.6
  0.7 0.7 %copy-done.7 = s32[1,4,4]{2,1,0:T(4,128)S(1)} copy-done((s32[1,4,4]{2,1,0:T(4,128)S(1)}, s32[1,4,4]{2,1,0:T(4,128)}, u32[]{:S(2)}) %copy-start.7) | copy-done | bytes 88
  1.3 0.0 copy-done.6
  1.3 0.0 copy-start.8
  1.3 0.0 copy-start.9
  1.4 0.7 %copy-done.8 = f32[1,4,4]{2,1,0:T(4,128)S(1)} copy-done((f32[1,4,4]{2,1,0:T(4,128)S(1)}, f32[1,4,4]{2,1,0:T(4,128)}, u32[]{:S(2)}) %copy-start.8) | copy-done | bytes 88
  2.0 0.0 copy-done.9
  2.0 0.0 copy-start.4
  2.0 0.0 copy-start.5
  2.1 0.6 %copy-done.4 = s32[1,4]{1,0:T(1,128)S(1)} copy-done((s32[1,4]{1,0:T(1,128)S(1)}, s32[1,4]{1,0:T(1,128)}, u32[]{:S(2)}) %copy-start.4) | copy-done | bytes 40
  2.7 0.0 copy-done.5
  2.7 0.0 copy-start
  2.7 0.9 %copy-done = bf16[1,32,8,512]{3,2,1,0:T(8,128)(2,1)S(1)} copy-done((bf16[1,32,8,512]{3,2,1,0:T(8,128)(2,1)S(1)}, bf16[1,32,8,512]{3,2,1,0:T(8,128)(2,1)}, u32[]{:S(2)}) %copy-start) | copy-done | bytes 262168
  3.7 0.0 copy-start.1
  3.7 0.9 %copy-done.1 = bf16[1,8,4,4,512]{4,3,2,1,0:T(4,128)(2,1)S(1)} copy-done((bf16[1,8,4,4,512]{4,3,2,1,0:T(4,128)(2,1)S(1)}, bf16[1,8,4,4,512]{4,3,2,1,0:T(4,128)(2,1)}, u32[]{:S(2)}) %copy-start.1) | copy-done | bytes 131096
  4.6 0.0 copy-start.2
  4.6 0.8 %copy-done.2 = bf16[8,32,3,3,3]{1,0,4,3,2:T(8,128)(2,1)S(1)} copy-done((bf16[8,32,3,3,3]{1,0,4,3,2:T(8,128)(2,1)S(1)}, bf16[8,32,3,3,3]{1,0,4,3,2:T(8,128)(2,1)}, u32[]{:S(2)}) %copy-start.2) | copy-done | bytes 13848
  5.4 0.0 copy-start.3
  5.4 0.8 %copy-done.3 = bf16[8,8,3,3,3]{1,0,4,3,2:T(8,128)(2,1)S(1)} copy-done((bf16[8,8,3,3,3]{1,0,4,3,2:T(8,128)(2,1)S(1)}, bf16[8,8,3,3,3]{1,0,4,3,2:T(8,128)(2,1)}, u32[]{:S(2)}) %copy-start.3) | copy-done | bytes 3480
  6.2 45.6 %core.1 = (f32[128,512]{1,0:T(8,128)S(1)}, f32[72,128]{1,0:T(8,128)S(1)}) custom-call(bf16[32,8,512]{2,1,0:T(8,128)(2,1)S(1)} %bitcast.23, bf16[8,4,4,512]{3,2,1,0:T(4,128)(2,1)S(1)} %bitcast.25, s32[8,128]{1,0:T(8,128)S(1)} %pad.8.ints_ref, f32[8,128]{1,0:T(8,128)S(1)} %select_maximum_fusion.floats_ref, s32[4]{0:T(128)S(1)} %bitcast.28, f32[8]{0:T(128)S(1)} %copy-done.5, ...), custom_call_target="tpu_custom_call" | custom-call | tf_op jit(solution)/shard_map/core/pallas_call | solution.py:469
  51.8 0.9 %copy.18 = f32[8,16,512]{2,0,1:T(8,128)} copy(f32[8,16,512]{2,1,0:T(8,128)S(1)} %bitcast.24) | data formatting | bytes 524288 | tf_op jit(solution)/shard_map/reshape | solution.py:526
  52.6 0.1 slice.17
  52.7 0.1 reshape.21
  52.8 0.7 %copy.16 = f32[8,8,3,3,3]{1,0,4,3,2:T(8,128)} copy(f32[8,8,3,3,3]{1,3,0,4,2:T(4,128)S(1)} %bitcast.29) | data formatting | bytes 13824
  53.5 0.1 reshape.20
  53.6 0.7 %copy.15 = f32[8,32,3,3,3]{1,0,4,3,2:T(8,128)} copy(f32[8,32,3,3,3]{1,3,0,4,2:T(4,128)S(1)} %bitcast.30) | data formatting | bytes 55296
  (6 shorter events, 0.0 us)
Async XLA Ops:
  0.6 0.7 %copy-start.7 = (s32[1,4,4]{2,1,0:T(4,128)S(1)}, s32[1,4,4]{2,1,0:T(4,128)}, u32[]{:S(2)}) copy-start(s32[1,4,4]{2,1,0:T(4,128)} %param.12) | copy-start | bytes 196
  0.6 0.7 %copy-start.6 = (s32[1,4,4]{2,1,0:T(4,128)S(1)}, s32[1,4,4]{2,1,0:T(4,128)}, u32[]{:S(2)}) copy-start(s32[1,4,4]{2,1,0:T(4,128)} %param.14) | copy-start | bytes 196
  1.3 0.7 %copy-start.8 = (f32[1,4,4]{2,1,0:T(4,128)S(1)}, f32[1,4,4]{2,1,0:T(4,128)}, u32[]{:S(2)}) copy-start(f32[1,4,4]{2,1,0:T(4,128)} %param.15) | copy-start | bytes 196
  1.3 0.7 %copy-start.9 = (f32[1,4,4]{2,1,0:T(4,128)S(1)}, f32[1,4,4]{2,1,0:T(4,128)}, u32[]{:S(2)}) copy-start(f32[1,4,4]{2,1,0:T(4,128)} %param.13) | copy-start | bytes 196
  2.0 0.7 %copy-start.4 = (s32[1,4]{1,0:T(1,128)S(1)}, s32[1,4]{1,0:T(1,128)}, u32[]{:S(2)}) copy-start(s32[1,4]{1,0:T(1,128)} %param.11) | copy-start | bytes 52
  2.0 0.7 %copy-start.5 = (f32[8]{0:T(128)S(1)}, f32[8]{0:T(128)}, u32[]{:S(2)}) copy-start(f32[8]{0:T(128)} %bias_ref.1) | copy-start | bytes 100
  2.7 0.9 %copy-start = (bf16[1,32,8,512]{3,2,1,0:T(8,128)(2,1)S(1)}, bf16[1,32,8,512]{3,2,1,0:T(8,128)(2,1)}, u32[]{:S(2)}) copy-start(bf16[1,32,8,512]{3,2,1,0:T(8,128)(2,1)} %param.10) | copy-start | bytes 786436
  3.7 0.9 %copy-start.1 = (bf16[1,8,4,4,512]{4,3,2,1,0:T(4,128)(2,1)S(1)}, bf16[1,8,4,4,512]{4,3,2,1,0:T(4,128)(2,1)}, u32[]{:S(2)}) copy-start(bf16[1,8,4,4,512]{4,3,2,1,0:T(4,128)(2,1)} %param.19) | copy-start | bytes 393220
  4.6 0.8 %copy-start.2 = (bf16[8,32,3,3,3]{1,0,4,3,2:T(8,128)(2,1)S(1)}, bf16[8,32,3,3,3]{1,0,4,3,2:T(8,128)(2,1)}, u32[]{:S(2)}) copy-start(bf16[8,32,3,3,3]{1,0,4,3,2:T(8,128)(2,1)} %param.16) | copy-start | bytes 41476
  5.4 0.8 %copy-start.3 = (bf16[8,8,3,3,3]{1,0,4,3,2:T(8,128)(2,1)S(1)}, bf16[8,8,3,3,3]{1,0,4,3,2:T(8,128)(2,1)}, u32[]{:S(2)}) copy-start(bf16[8,8,3,3,3]{1,0,4,3,2:T(8,128)(2,1)} %param.18) | copy-start | bytes 10372

commit v4 on v3

--- a/solution.py
+++ b/solution.py
@@ -9,7 +9,7 @@
 
 view_offsets = (-2, -1, 1, 2)
 MESH = pl.DeviceIdType.MESH
-SMEM = pl.BlockSpec(memory_space=pltpu.SMEM)
+HBM = pl.BlockSpec(memory_space=pltpu.HBM)
 VMEM = pl.BlockSpec(memory_space=pltpu.VMEM)
 
 
@@ -46,17 +46,36 @@
                 [x[:, before : before + 128], x[:, start : start + 256], x[:, after : after + 128]], axis=1
             )
         )
-    source = lax.broadcasted_iota(jnp.int32, (512, 256), 0) - 128
-    target = lax.broadcasted_iota(jnp.int32, (512, 256), 1)
-    pick = jnp.where(source - target == by, 1.0, 0.0).astype(x.dtype)
+    apart = lax.broadcasted_iota(jnp.int32, (128, 128), 0) - lax.broadcasted_iota(jnp.int32, (128, 128), 1)
+    low, mid, high = (jnp.where(apart == by - d, 1.0, 0.0).astype(x.dtype) for d in (-128, 0, 128))
+    none = jnp.zeros_like(mid)
+    pick = jnp.concatenate(
+        [jnp.concatenate([low, mid, high, none], axis=0), jnp.concatenate([none, low, mid, high], axis=0)], axis=1
+    )
     out = mul(jnp.concatenate(parts, axis=0), pick)
     return jnp.concatenate([out[i * count : (i + 1) * count] for i in range(width // 256)], axis=1)
 
 
+def in_steps(count, size, body):
+    if count % size:
+        size = 1
+
+    def step(i, _):
+        for n in range(size):
+            body(i * size + n, 0)
+        return 0
+
+    if count == size:
+        step(0, 0)
+    else:
+        lax.fori_loop(0, count // size, step, 0)
+
+
 def compute(
     dims,
-    raw_ref, cotangent_ref, ints_ref, floats_ref, mask_ref, bias_ref, w1_ref, w2_ref,
+    raw_hbm, cotangent_hbm, row_hbm, col_hbm, fy_hbm, fx_hbm, mask_hbm, bias_hbm, w1_hbm, w2_hbm,
     grad_ref, wsum_ref,
+    raw_ref, cotangent_ref, mask_ref, bias_ref, w1_ref, w2_ref,
     bands, halo, ints_in, floats_in, ints, floats,
     warp, mean, cost, scot, spre, hid, acc1, acc2, cg, pad, taps,
     own_grad, out_grad, a_send, a_recv, b_send, b_recv, c_send, c_recv, ar, ar_in,
@@ -92,11 +111,26 @@
         reach *= 2
     partners.append((cam, other))
 
+    fetches = [
+        pltpu.make_async_copy(src, dst, local_sem.at[n])
+        for n, (src, dst) in enumerate(
+            [
+                (raw_hbm, raw_ref), (cotangent_hbm, cotangent_ref), (w1_hbm, w1_ref), (w2_hbm, w2_ref),
+                (row_hbm, ints.at[me, 0]), (col_hbm, ints.at[me, 1]),
+                (fy_hbm, floats.at[me, 0]), (fx_hbm, floats.at[me, 1]),
+                (mask_hbm, mask_ref), (bias_hbm, bias_ref),
+            ]
+        )
+    ]
+    for fetch in fetches:
+        fetch.start()
+
     barrier = pltpu.get_barrier_semaphore()
     greeted = [(at(-2), me), (at(-1), me), (at(1), me), (at(2), me)] + partners
     for device in greeted:
         pl.semaphore_signal(barrier, inc=1, device_id=device, device_id_type=MESH)
 
+    fetches[0].wait()
     wide[...] = raw_ref[...].astype(jnp.float32)
     for r in range(held):
         feat_ref[r * chans : (r + 1) * chans, :] = wide[:, r, :].astype(feat_ref.dtype)
@@ -124,13 +158,15 @@
     feat1 = begin(remote(4, part(feat_ref, me), part(bands.at[1], me), (at(1), me)))
     feat0 = begin(remote(3, part(feat_ref, me), part(bands.at[0], me), (at(-2), me)))
     feat2 = begin(remote(5, feat_ref, bands.at[2], (mate, me)))
-    ints_copy = begin(remote(0, ints_ref, ints_in, (cam, other)))
-    floats_copy = begin(remote(1, floats_ref, floats_in, (cam, other)))
-    own_ints = pltpu.make_async_copy(ints_ref, ints.at[me], local_sem.at[0])
-    own_floats = pltpu.make_async_copy(floats_ref, floats.at[me], local_sem.at[1])
-    own_ints.start()
-    own_floats.start()
-
+    scalar_copies = [
+        begin(remote(n, src, dst, (cam, other)))
+        for n, src, dst in (
+            (0, row_hbm, ints_in.at[0]), (1, col_hbm, ints_in.at[1]),
+            (17, fy_hbm, floats_in.at[0]), (18, fx_hbm, floats_in.at[1]),
+        )
+    ]
+
+    fetches[1].wait()
     for i in range(own):
         cot_wide[:, i * height : (i + 1) * height, :] = cotangent_ref[:, i].astype(jnp.float32)
     for i in range(own):
@@ -171,6 +207,8 @@
             found.append(total)
         return found
 
+    for fetch in fetches[2:]:
+        fetch.wait()
     for kd in range(3):
         for kw in range(3):
             for h, value in enumerate(blocks(w1_ref, chans, kd, kw)):
@@ -189,28 +227,27 @@
     which = lax.rem(lax.broadcasted_iota(jnp.int32, (mband, width), 0), mid)
     column = jnp.zeros((mband, width), jnp.float32)
     for o in range(mid):
-        column = jnp.where(which == o, bias_ref[o], column)
+        column = jnp.where(which == o, bias_ref[0, o], column)
     bias[...] = column
 
     def weight_of(s):
-        return mask_ref[s].astype(jnp.float32)
+        return mask_ref[0, s].astype(jnp.float32)
 
     count = 1.0 + weight_of(0) + weight_of(1) + weight_of(2) + weight_of(3)
     inv = 1.0 / jnp.full((1, width), count, jnp.float32)
 
-    own_ints.wait()
-    own_floats.wait()
-    ints_copy.wait_recv()
-    floats_copy.wait_recv()
-    more_ints = pltpu.make_async_copy(ints_in, ints.at[other], local_sem.at[2])
-    more_floats = pltpu.make_async_copy(floats_in, floats.at[other], local_sem.at[3])
-    more_ints.start()
-    more_floats.start()
+    arrivals = []
+    for n, (src, dst) in enumerate(
+        [(ints_in, ints), (ints_in, ints), (floats_in, floats), (floats_in, floats)]
+    ):
+        scalar_copies[n].wait_recv()
+        arrivals.append(pltpu.make_async_copy(src.at[n % 2], dst.at[other, n % 2], local_sem.at[10 + n]))
+        arrivals[-1].start()
     halo_copy.wait_recv()
     for i in range(2):
         shift_plane(halo[i * mband : (i + 1) * mband, :], own * other + i)
-    more_ints.wait()
-    more_floats.wait()
+    for arrival in arrivals:
+        arrival.wait()
 
     def place(p):
         at_plane = p + me * (2 * own - planes)
@@ -218,13 +255,13 @@
 
     def row_of(s, p):
         slab, lane = place(p)
-        return ints[slab, s, lane]
+        return ints[slab, 0, s, lane]
 
     def weights(s, p):
         slab, lane = place(p)
-        c = ints[slab, s + 4, lane]
-        fy = floats[slab, s, lane]
-        fx = floats[slab, s + 4, lane]
+        c = ints[slab, 1, s, lane]
+        fy = floats[slab, 0, s, lane]
+        fx = floats[slab, 1, s, lane]
         spot = lanes(width) + c
         left = jnp.where((spot >= 0) & (spot < width), 1.0 - fx, 0.0)
         right = jnp.where((spot >= -1) & (spot < width - 1), fx, 0.0)
@@ -260,7 +297,7 @@
                     cost[pl.ds(spot, chans), :] = (second * inv - average * average).astype(cost.dtype)
             return 0
 
-        lax.fori_loop(0, planes, plane, 0)
+        in_steps(planes, 2, plane)
 
     feat2.wait_recv()
     warp_slot(2, False)
@@ -294,7 +331,7 @@
         spre[pl.ds(base + 2 * mband, mband), :] = from_right(back).astype(spre.dtype)
         return 0
 
-    lax.fori_loop(0, own + (planes - own) // 2, middle, 0)
+    in_steps(own + (planes - own) // 2, own + (planes - own) // 2, middle)
 
     acc1[...] = jnp.zeros_like(acc1)
     acc2[...] = jnp.zeros_like(acc2)
@@ -309,7 +346,7 @@
         acc2[:, :mband] += mul_t(c3, hid[pl.ds(pl.multiple_of(p * mband, mband), mband), :])
         return 0
 
-    lax.fori_loop(0, own, back_plane, 0)
+    in_steps(own, 2, back_plane)
 
     def fold(acc, block, offset):
         rows = acc[...].reshape(9, height, mid, 128)
@@ -330,7 +367,7 @@
     def reduce_begin():
         k = len(reduce_copies)
         if k < steps:
-            reduce_copies.append(begin(remote(17 + k, ar.at[k], ar_in.at[k], partners[k])))
+            reduce_copies.append(begin(remote(19 + k, ar.at[k], ar_in.at[k], partners[k])))
 
     def reduce_next():
         k = len(reduce_copies)
@@ -363,7 +400,7 @@
             pad[i, height * chans :, :] = carried
             return 0
 
-        lax.fori_loop(0, own, plane, 0)
+        in_steps(own, 2, plane)
         starts = [row_of(s, first_own + i) for i in range(own)]
         for r in range(held):
             total = None
@@ -456,9 +493,6 @@
     planes = own + 2
     steps = cams.bit_length()
 
-    wide = ((0, 0), (0, 128 - own))
-    ints = jnp.pad(jnp.concatenate([row_offset[0], col_offset[0]]), wide)
-    floats = jnp.pad(jnp.concatenate([frac_row[0], frac_col[0]]), wide)
     order = (2, 3, 4, 0, 1)
     w1 = jnp.transpose(first_kernel, order)
     w2 = jnp.transpose(second_kernel, order)
@@ -472,15 +506,21 @@
             jax.ShapeDtypeStruct((rows, width), f32),
             jax.ShapeDtypeStruct((9 * mid, 128), f32),
         ),
-        in_specs=[VMEM] * 4 + [SMEM] * 2 + [VMEM] * 2,
+        in_specs=[HBM] * 10,
         out_specs=(VMEM, VMEM),
         scratch_shapes=[
+            pltpu.VMEM(features.shape[1:], bf16),
+            pltpu.VMEM(cotangent.shape[1:], bf16),
+            pltpu.SMEM((1, 4), i32),
+            pltpu.SMEM((1, mid), f32),
+            pltpu.VMEM(w1.shape, bf16),
+            pltpu.VMEM(w2.shape, bf16),
             pltpu.VMEM((4, held * chans, width), bf16),
             pltpu.VMEM((2 * mband, width), bf16),
-            pltpu.VMEM((8, 128), i32),
-            pltpu.VMEM((8, 128), f32),
-            pltpu.SMEM((2, 8, 128), i32),
-            pltpu.SMEM((2, 8, 128), f32),
+            pltpu.VMEM((2, 4, own), i32),
+            pltpu.VMEM((2, 4, own), f32),
+            pltpu.SMEM((2, 2, 4, own), i32),
+            pltpu.SMEM((2, 2, 4, own), f32),
             pltpu.VMEM((4, planes, band, width), f32),
             pltpu.VMEM((planes, band, width), f32),
             pltpu.VMEM(((planes + 2) * band, width), bf16),
@@ -513,15 +553,18 @@
             pltpu.VMEM((band, taps_rows), bf16),
             pltpu.VMEM((taps_rows, 128), f32),
             pltpu.VMEM((mband, width), f32),
-            pltpu.SemaphoreType.DMA((17 + steps,)),
-            pltpu.SemaphoreType.DMA((17 + steps,)),
-            pltpu.SemaphoreType.DMA((4,)),
+            pltpu.SemaphoreType.DMA((19 + steps,)),
+            pltpu.SemaphoreType.DMA((19 + steps,)),
+            pltpu.SemaphoreType.DMA((14,)),
         ],
         compiler_params=pltpu.CompilerParams(
             vmem_limit_bytes=48 * 2**20, collective_id=0, has_side_effects=True
         ),
         name="core",
-    )(features[0], cotangent[0], ints, floats, view_mask[0], first_bias, w1, w2)
+    )(
+        features[0], cotangent[0], row_offset[0], col_offset[0], frac_row[0], frac_col[0],
+        view_mask, first_bias[None], w1, w2,
+    )
 
     feature_grad = jnp.transpose(grads.reshape(held, half, width), (1, 0, 2))
     scale = (cams * slabs * own * height * width) ** (-0.5)

time: 54.6 us -> 49.5 us (0.907)
  Pallas kernels: 45.6 us -> 41.8 us
  local copies, waits for them, and re-layouts: 7.98 us -> 6.65 us
    pallas_call x1, Pallas kernels: 45.6 us -> 41.8 us  [shards(): pl.pallas_call(functools.partial(compute, (chans, mid, height, held, widt...]
    unnamed x22, local copies, waits for them, and re-layouts: 6.8 us -> 5.47 us
where the time goes in v4:
time: 49.5 us; the launch traced here: 49.2 us
  Pallas kernels  41.8 us (84%)
  local copies, waits for them, and re-layouts  6.65 us (13%)
  between operations  0.72 us (1%)
    pallas_call x1, Pallas kernels, shards(): pl.pallas_call(functools.partial(compute, (chans, mid, height, held, widt...  41.8 us
    unnamed x22, local copies, waits for them, and re-layouts  5.47 us

profile of v4, /device:TPU:0, one launch (start us, length us, event | category | flops | bytes accessed | tf_op | source)
XLA Modules:
  0.0 49.2 jit_solution(18352130937470317096)
XLA Ops:
  0.6 0.0 copy-start.7
  0.6 0.0 copy-start.6
  0.7 0.0 copy-start.5
  0.7 0.0 copy-start.4
  0.7 0.0 copy-start.8
  0.7 0.0 copy-start.9
  0.7 0.6 %copy-done.7 = f32[1,4,4]{2,1,0:T(4,128)S(1)} copy-done((f32[1,4,4]{2,1,0:T(4,128)S(1)}, f32[1,4,4]{2,1,0:T(4,128)}, u32[]{:S(2)}) %copy-start.7) | copy-done | bytes 88
  1.3 0.0 copy-done.6
  1.3 0.0 copy-done.5
  1.3 0.0 copy-done.4
  1.4 0.0 copy-done.8
  1.4 0.0 copy-done.9
  1.4 0.0 copy-start
  1.4 0.9 %copy-done = bf16[1,32,8,512]{3,2,1,0:T(8,128)(2,1)S(1)} copy-done((bf16[1,32,8,512]{3,2,1,0:T(8,128)(2,1)S(1)}, bf16[1,32,8,512]{3,2,1,0:T(8,128)(2,1)}, u32[]{:S(2)}) %copy-start) | copy-done | bytes 262168
  2.3 0.0 copy-start.1
  2.3 0.9 %copy-done.1 = bf16[1,8,4,4,512]{4,3,2,1,0:T(4,128)(2,1)S(1)} copy-done((bf16[1,8,4,4,512]{4,3,2,1,0:T(4,128)(2,1)S(1)}, bf16[1,8,4,4,512]{4,3,2,1,0:T(4,128)(2,1)}, u32[]{:S(2)}) %copy-start.1) | copy-done | bytes 131096
  3.2 0.0 copy-start.2
  3.2 0.8 %copy-done.2 = bf16[8,32,3,3,3]{1,0,4,3,2:T(8,128)(2,1)S(1)} copy-done((bf16[8,32,3,3,3]{1,0,4,3,2:T(8,128)(2,1)S(1)}, bf16[8,32,3,3,3]{1,0,4,3,2:T(8,128)(2,1)}, u32[]{:S(2)}) %copy-start.2) | copy-done | bytes 13848
  4.0 0.0 copy-start.3
  4.0 0.8 %copy-done.3 = bf16[8,8,3,3,3]{1,0,4,3,2:T(8,128)(2,1)S(1)} copy-done((bf16[8,8,3,3,3]{1,0,4,3,2:T(8,128)(2,1)S(1)}, bf16[8,8,3,3,3]{1,0,4,3,2:T(8,128)(2,1)}, u32[]{:S(2)}) %copy-start.3) | copy-done | bytes 3480
  4.9 41.8 %core.1 = (f32[128,512]{1,0:T(8,128)S(1)}, f32[72,128]{1,0:T(8,128)S(1)}) custom-call(bf16[32,8,512]{2,1,0:T(8,128)(2,1)S(1)} %bitcast.23, bf16[8,4,4,512]{3,2,1,0:T(4,128)(2,1)S(1)} %bitcast.25, s32[4,4]{1,0:T(4,128)S(1)} %bitcast.28, s32[4,4]{1,0:T(4,128)S(1)} %bitcast.29, f32[4,4]{1,0:T(4,128)S(1)} %bitcast.30, f32[4,4]{1,0:T(4,128)S(1)} %bitcast.31, ...), custom_call_target="tpu_custom_call" | custom-call | tf_op jit(solution)/shard_map/core/pallas_call | solution.py:503
  46.7 0.9 %copy.18 = f32[8,16,512]{2,0,1:T(8,128)} copy(f32[8,16,512]{2,1,0:T(8,128)S(1)} %bitcast.24) | data formatting | bytes 524288 | tf_op jit(solution)/shard_map/reshape | solution.py:569
  47.5 0.1 slice.17
  47.6 0.1 reshape.21
  47.7 0.7 %copy.16 = f32[8,8,3,3,3]{1,0,4,3,2:T(8,128)} copy(f32[8,8,3,3,3]{1,3,0,4,2:T(4,128)S(1)} %bitcast.33) | data formatting | bytes 13824
  48.4 0.1 reshape.20
  48.5 0.7 %copy.15 = f32[8,32,3,3,3]{1,0,4,3,2:T(8,128)} copy(f32[8,32,3,3,3]{1,3,0,4,2:T(4,128)S(1)} %bitcast.34) | data formatting | bytes 55296
  (3 shorter events, 0.0 us)
Async XLA Ops:
  0.6 0.7 %copy-start.7 = (f32[1,4,4]{2,1,0:T(4,128)S(1)}, f32[1,4,4]{2,1,0:T(4,128)}, u32[]{:S(2)}) copy-start(f32[1,4,4]{2,1,0:T(4,128)} %param.15) | copy-start | bytes 196
  0.6 0.7 %copy-start.6 = (f32[1,4,4]{2,1,0:T(4,128)S(1)}, f32[1,4,4]{2,1,0:T(4,128)}, u32[]{:S(2)}) copy-start(f32[1,4,4]{2,1,0:T(4,128)} %param.13) | copy-start | bytes 196
  0.7 0.7 %copy-start.5 = (s32[1,4,4]{2,1,0:T(4,128)S(1)}, s32[1,4,4]{2,1,0:T(4,128)}, u32[]{:S(2)}) copy-start(s32[1,4,4]{2,1,0:T(4,128)} %param.14) | copy-start | bytes 196
  0.7 0.7 %copy-start.4 = (s32[1,4,4]{2,1,0:T(4,128)S(1)}, s32[1,4,4]{2,1,0:T(4,128)}, u32[]{:S(2)}) copy-start(s32[1,4,4]{2,1,0:T(4,128)} %param.12) | copy-start | bytes 196
  0.7 0.7 %copy-start.8 = (s32[1,4]{1,0:T(1,128)S(1)}, s32[1,4]{1,0:T(1,128)}, u32[]{:S(2)}) copy-start(s32[1,4]{1,0:T(1,128)} %mask_hbm.1) | copy-start | bytes 52
  0.7 0.7 %copy-start.9 = (f32[8]{0:T(128)S(1)}, f32[8]{0:T(128)}, u32[]{:S(2)}) copy-start(f32[8]{0:T(128)} %param.17) | copy-start | bytes 100
  1.4 1.0 %copy-start = (bf16[1,32,8,512]{3,2,1,0:T(8,128)(2,1)S(1)}, bf16[1,32,8,512]{3,2,1,0:T(8,128)(2,1)}, u32[]{:S(2)}) copy-start(bf16[1,32,8,512]{3,2,1,0:T(8,128)(2,1)} %param.10) | copy-start | bytes 786436
  2.3 0.9 %copy-start.1 = (bf16[1,8,4,4,512]{4,3,2,1,0:T(4,128)(2,1)S(1)}, bf16[1,8,4,4,512]{4,3,2,1,0:T(4,128)(2,1)}, u32[]{:S(2)}) copy-start(bf16[1,8,4,4,512]{4,3,2,1,0:T(4,128)(2,1)} %param.19) | copy-start | bytes 393220
  3.2 0.8 %copy-start.2 = (bf16[8,32,3,3,3]{1,0,4,3,2:T(8,128)(2,1)S(1)}, bf16[8,32,3,3,3]{1,0,4,3,2:T(8,128)(2,1)}, u32[]{:S(2)}) copy-start(bf16[8,32,3,3,3]{1,0,4,3,2:T(8,128)(2,1)} %param.16) | copy-start | bytes 41476
  4.0 0.8 %copy-start.3 = (bf16[8,8,3,3,3]{1,0,4,3,2:T(8,128)(2,1)S(1)}, bf16[8,8,3,3,3]{1,0,4,3,2:T(8,128)(2,1)}, u32[]{:S(2)}) copy-start(bf16[8,8,3,3,3]{1,0,4,3,2:T(8,128)(2,1)} %param.18) | copy-start | bytes 10372

commit v5 on v4

--- a/solution.py
+++ b/solution.py
@@ -297,7 +297,7 @@
                     cost[pl.ds(spot, chans), :] = (second * inv - average * average).astype(cost.dtype)
             return 0
 
-        in_steps(planes, 2, plane)
+        in_steps(planes, 3, plane)
 
     feat2.wait_recv()
     warp_slot(2, False)
@@ -346,7 +346,7 @@
         acc2[:, :mband] += mul_t(c3, hid[pl.ds(pl.multiple_of(p * mband, mband), mband), :])
         return 0
 
-    in_steps(own, 2, back_plane)
+    in_steps(own, 4, back_plane)
 
     def fold(acc, block, offset):
         rows = acc[...].reshape(9, height, mid, 128)
@@ -400,7 +400,7 @@
             pad[i, height * chans :, :] = carried
             return 0
 
-        in_steps(own, 2, plane)
+        in_steps(own, 4, plane)
         starts = [row_of(s, first_own + i) for i in range(own)]
         for r in range(held):
             total = None
@@ -558,7 +558,7 @@
             pltpu.SemaphoreType.DMA((14,)),
         ],
         compiler_params=pltpu.CompilerParams(
-            vmem_limit_bytes=48 * 2**20, collective_id=0, has_side_effects=True
+            vmem_limit_bytes=62 * 2**20, collective_id=0, has_side_effects=True
         ),
         name="core",
     )(

time: 49.5 us -> 45.5 us (0.919)
  the two profiles are of different devices: /device:TPU:0 before, /device:TPU:2 now
where the time goes in v5:
time: 45.5 us; the launch traced here: 45.3 us
  Pallas kernels  41.2 us (91%)
  local copies, waits for them, and re-layouts  3.44 us (8%)
  between operations  0.68 us (1%)
    pallas_call x1, Pallas kernels, shards(): pl.pallas_call(functools.partial(compute, (chans, mid, height, held, widt...  41.2 us
    reshape x1, local copies, waits for them, and re-layouts, shards(): feature_grad = jnp.transpose(grads.reshape(held, half, width), (1, 0, 2))  1.82 us
    unnamed x4, local copies, waits for them, and re-layouts  1.31 us

profile of v5, /device:TPU:2, one launch (start us, length us, event | category | flops | bytes accessed | tf_op | source)
XLA Modules:
  0.0 45.3 jit_solution(6897989002030497953)
XLA Ops:
  0.6 41.2 %core.1 = (f32[128,512]{1,0:T(8,128)}, f32[72,128]{1,0:T(8,128)}) custom-call(bf16[32,8,512]{2,1,0:T(8,128)(2,1)} %bitcast.27, bf16[8,4,4,512]{3,2,1,0:T(4,128)(2,1)} %bitcast.30, s32[4,4]{1,0:T(4,128)} %bitcast.33, s32[4,4]{1,0:T(4,128)} %bitcast.34, f32[4,4]{1,0:T(4,128)} %bitcast.35, f32[4,4]{1,0:T(4,128)} %bitcast.36, s32[1,4]{1,0:T(1,128)} %mask_hbm.1, ...), custom_call_target="tpu_custom_call" | custom-call | tf_op jit(solution)/shard_map/core/pallas_call | solution.py:503
  41.8 0.0 copy-start
  41.8 1.8 %copy.18 = f32[8,16,512]{2,0,1:T(8,128)} copy(f32[8,16,512]{2,1,0:T(8,128)} %bitcast.29) | data formatting | bytes 524288 | tf_op jit(solution)/shard_map/reshape | solution.py:569
  43.7 0.0 copy-done
  43.7 0.1 slice.17
  43.8 0.1 reshape.21
  43.9 0.7 %copy.16 = f32[8,8,3,3,3]{1,0,4,3,2:T(8,128)} copy(f32[8,8,3,3,3]{1,3,0,4,2:T(4,128)S(1)} %bitcast.23) | data formatting | bytes 13824
  44.5 0.1 reshape.20
  44.7 0.7 %copy.15 = f32[8,32,3,3,3]{1,0,4,3,2:T(8,128)} copy(f32[8,32,3,3,3]{1,3,0,4,2:T(4,128)S(1)} %bitcast.24) | data formatting | bytes 55296
  (3 shorter events, 0.0 us)
Async XLA Ops:
  41.8 1.8 %copy-start = (f32[72,128]{1,0:T(8,128)S(1)}, f32[72,128]{1,0:T(8,128)}, u32[]{:S(2)}) copy-start(f32[72,128]{1,0:T(8,128)} %get-tuple-element.6) | copy-start | bytes 110596

commit v6 on v5

--- a/solution.py
+++ b/solution.py
@@ -475,7 +475,10 @@
     own_grad[me] = own_grad[me] + a_recv[0, me].astype(jnp.float32) + b_recv[2].astype(jnp.float32)
     c0.wait_recv()
     c1.wait_recv()
-    grad_ref[...] = own_grad[me] + (c_recv[0].astype(jnp.float32) + c_recv[1].astype(jnp.float32))
+    for r in range(held):
+        rows = slice(r * half, (r + 1) * half)
+        landed = c_recv[0, rows, :].astype(jnp.float32) + c_recv[1, rows, :].astype(jnp.float32)
+        grad_ref[:, r, :] = own_grad[me, rows, :] + landed
     for copy in started:
         copy.wait_send()
 
@@ -503,7 +506,7 @@
     grads, wsum = pl.pallas_call(
         functools.partial(compute, (chans, mid, height, held, width, own, planes, cams)),
         out_shape=(
-            jax.ShapeDtypeStruct((rows, width), f32),
+            jax.ShapeDtypeStruct((half, held, width), f32),
             jax.ShapeDtypeStruct((9 * mid, 128), f32),
         ),
         in_specs=[HBM] * 10,
@@ -566,13 +569,12 @@
         view_mask, first_bias[None], w1, w2,
     )
 
-    feature_grad = jnp.transpose(grads.reshape(held, half, width), (1, 0, 2))
     scale = (cams * slabs * own * height * width) ** (-0.5)
     taps = (wsum * scale).reshape(3, 3, mid, 128)[::-1, ::-1]
     first = taps[..., : 3 * chans].reshape(3, 3, mid, 3, chans)
     second = taps[..., 3 * chans : 3 * chans + 3 * mid].reshape(3, 3, mid, 3, mid)
     order = (2, 4, 0, 3, 1)
-    return feature_grad[None], jnp.transpose(first, order), jnp.transpose(second, order)
+    return grads[None], jnp.transpose(first, order), jnp.transpose(second, order)
 
 
 def solution(mesh):

time: 45.5 us -> 45.4 us (level)
  local copies, waits for them, and re-layouts: 3.44 us -> 2.5 us
  other arithmetic: 0.01 us -> 0.77 us
    reshape x1 -> x0, local copies, waits for them, and re-layouts: 1.82 us -> none  [shards(): feature_grad = jnp.transpose(grads.reshape(held, half, width), (1, 0, 2))]
    unnamed x4 -> x5, local copies, waits for them, and re-layouts: 1.31 us -> 2.19 us
    mul x1, other arithmetic: 0.01 us -> 0.77 us  [shards(): taps = (wsum * scale).reshape(3, 3, mid, 128)[::-1, ::-1]]
where the time goes in v6:
time: 45.4 us; the launch traced here: 45.2 us
  Pallas kernels  41.2 us (91%)
  local copies, waits for them, and re-layouts  2.5 us (6%)
  other arithmetic  0.77 us (2%)
  between operations  0.66 us (1%)
    pallas_call x1, Pallas kernels, shards(): pl.pallas_call(functools.partial(compute, (chans, mid, height, held, widt...  41.2 us
    unnamed x5, local copies, waits for them, and re-layouts  2.19 us

profile of v6, /device:TPU:2, one launch (start us, length us, event | category | flops | bytes accessed | tf_op | source)
XLA Modules:
  0.0 45.2 jit_solution(17474519614905359907)
XLA Ops:
  0.6 41.2 %core.1 = (f32[16,8,512]{2,1,0:T(8,128)}, f32[72,128]{1,0:T(8,128)}) custom-call(bf16[32,8,512]{2,1,0:T(8,128)(2,1)} %bitcast.22, bf16[8,4,4,512]{3,2,1,0:T(4,128)(2,1)} %bitcast.24, s32[4,4]{1,0:T(4,128)} %bitcast.27, s32[4,4]{1,0:T(4,128)} %bitcast.28, f32[4,4]{1,0:T(4,128)} %bitcast.29, f32[4,4]{1,0:T(4,128)} %bitcast.30, s32[1,4]{1,0:T(1,128)} %mask_hbm.1, ...), custom_call_target="tpu_custom_call" | custom-call | tf_op jit(solution)/shard_map/core/pallas_call | solution.py:506
  41.9 0.8 %broadcast_multiply_fusion = f32[72,128]{1,0:T(8,128)S(1)} fusion(f32[72,128]{1,0:T(8,128)} %get-tuple-element.6), kind=kLoop, calls=%fused_computation | loop fusion | flops 9216 | bytes 73728 | tf_op jit(solution)/shard_map/mul | solution.py:573
  42.7 0.1 slice.17
  42.8 0.1 reshape.17
  42.9 0.7 %copy.14 = f32[8,8,3,3,3]{1,0,4,3,2:T(8,128)} copy(f32[8,8,3,3,3]{1,3,0,4,2:T(4,128)S(1)} %bitcast.18) | data formatting | bytes 13824
  43.5 0.0 copy-start
  43.5 0.1 reshape.16
  43.7 0.7 %copy.13 = f32[8,32,3,3,3]{1,0,4,3,2:T(8,128)} copy(f32[8,32,3,3,3]{1,3,0,4,2:T(4,128)S(1)} %bitcast.19) | data formatting | bytes 55296
  44.3 0.2 copy-done
  44.5 0.7 %copy.16 = f32[1,16,8,512]{3,2,1,0:T(8,128)} copy(f32[1,16,8,512]{3,2,1,0:T(8,128)S(1)} %bitcast.23) | data formatting | bytes 524288
  (2 shorter events, 0.0 us)
Async XLA Ops:
  43.5 0.9 %copy-start = (f32[16,8,512]{2,1,0:T(8,128)S(1)}, f32[16,8,512]{2,1,0:T(8,128)}, u32[]{:S(2)}) copy-start(f32[16,8,512]{2,1,0:T(8,128)} %get-tuple-element.5) | copy-start | bytes 786436
